TPU v7x, 32 devices: a whole 2x2x4 slice. The times are simulated.
32 devices in a mesh: rows: 16 (over z, y, core), rep: 2 (over x).
Axes of the slice: x: 2, y: 2, z: 4, core: 2. Of those that a mesh axis runs over, the one named last changes fastest.
Arguments:
- features: bfloat16 [8192, 128], P('rows'), may hold values from -6 to 6
- degree: int32 [8192], P('rows'), may hold values from 32 to 320
- tile_block: int32 [64, 16, 8], P('rows', 'rep'), may hold values from 0 to 3
- edge_count: int32 [64, 16, 8], P('rows', 'rep'), may hold values from 0 to 128, as said below
- edge_code: int32 [64, 16, 8, 128], P('rows', 'rep'), may hold values from 0 to 16368
- weight: bfloat16 [128, 256], replicated, may hold values from -3 to 3
- bias: float32 [256], replicated, may hold values from -3 to 3
- cotangent: bfloat16 [8192, 256], P(('rows', 'rep')), may hold values from -0.0625 to 0.0625
Outputs:
- activated: bfloat16 [8192, 256], P(('rows', 'rep'))
- grad_weight: float32 [128, 256], replicated
- grad_bias: float32 [256], replicated
Inputs may be any that keep to these rules, and one draw needn't show every extreme that they name: Only the first edge_count entries of a tile's edge codes are live; some tiles hold 128 live edges.
All inputs are finite; a program needn't handle non-finite values.
Results may differ from a plain program's by a relative error of at most 0.0063.
Values may be sent and summed in bfloat16 or wider, within the bound.
A program may use at most 64 MiB of HBM per device.

v0:
```python
import jax
import jax.numpy as jnp
from jax import lax
from jax.sharding import PartitionSpec as P


def from_behind(value, axis, steps):
    count = lax.axis_size(axis)
    pairs = [(source, (source + steps) % count) for source in range(count)]
    return lax.ppermute(value, axis, pairs)


def gelu_tanh(values):
    return jax.nn.gelu(values, approximate=True)


def tile_sums(buffer, offset, tile_block, edge_count, edge_code):
    block_ids = lax.dynamic_index_in_dim(tile_block, offset, 1, keepdims=False)
    live_count = lax.dynamic_index_in_dim(edge_count, offset, 1, keepdims=False)
    codes = lax.dynamic_index_in_dim(edge_code, offset, 1, keepdims=False)
    block_total, slot_count, edge_cap = codes.shape
    feat_width = buffer.shape[1]
    far_node = block_ids[:, :, None] * 128 + codes % 128
    picked = jnp.take(buffer, far_node.reshape(-1), axis=0).reshape(
        block_total, slot_count, edge_cap, feat_width
    )
    is_live = lax.broadcasted_iota(jnp.int32, codes.shape, 2) < live_count[:, :, None]
    target = jnp.where(is_live, codes // 128, -1)
    row_iota = lax.broadcasted_iota(jnp.int32, (1, 1, 128, 1), 2)
    onehot = (target[:, :, None, :] == row_iota).astype(jnp.bfloat16)
    summed = jnp.einsum("bkre,bkef->brf", onehot, picked, preferred_element_type=jnp.float32)
    return summed.reshape(block_total * 128, feat_width)


def local(features, degree, tile_block, edge_count, edge_code, weight, bias, cotangent):
    step_count = tile_block.shape[1]
    replicas = lax.axis_size("rep")
    replica = lax.axis_index("rep")
    inv_deg = lax.rsqrt(degree.astype(jnp.float32))
    scaled = (features.astype(jnp.float32) * inv_deg[:, None]).astype(jnp.bfloat16)

    def local_sums(buffer, offset):
        return tile_sums(buffer, offset, tile_block, edge_count, edge_code)

    buffer = scaled
    for bit_index in range(replicas.bit_length() - 1):
        shifted = from_behind(buffer, "rows", -(step_count << bit_index))
        select = replica // (1 << bit_index) % 2 == 1
        buffer = jnp.where(select, shifted, buffer)
    partial_total = local_sums(buffer, 0)

    def advance(step_index, loop_state):
        current, running = loop_state
        current = from_behind(current, "rows", -1)
        return (current, running + local_sums(current, step_index))

    buffer, partial_total = lax.fori_loop(1, step_count, advance, (buffer, partial_total))
    edge_sums = lax.psum_scatter(partial_total, "rep", scatter_dimension=0, tiled=True)
    share_rows = edge_sums.shape[0]
    share_start = replica * share_rows
    own_rows = lax.dynamic_slice_in_dim(scaled, share_start, share_rows, 0).astype(jnp.float32)
    own_inv = lax.dynamic_slice_in_dim(inv_deg, share_start, share_rows, 0)
    aggregate = (own_inv[:, None] * (edge_sums + own_rows)).astype(jnp.bfloat16)
    pre_act = jnp.dot(aggregate, weight, preferred_element_type=jnp.float32) + bias
    activated, pull_back = jax.vjp(gelu_tanh, pre_act)
    delta_bf = pull_back(cotangent.astype(jnp.float32))[0].astype(jnp.bfloat16)
    local_weight = lax.dot_general(
        aggregate, delta_bf, (((0,), (0,)), ((), ())), preferred_element_type=jnp.float32
    )
    local_bias = jnp.sum(delta_bf.astype(jnp.float32), axis=0)
    grad_weight, grad_bias = lax.psum((local_weight, local_bias), ("rows", "rep"))
    return (activated.astype(jnp.bfloat16), grad_weight, grad_bias)


def solution(mesh):
    in_specs = (
        P("rows", None),
        P("rows"),
        P("rows", "rep", None),
        P("rows", "rep", None),
        P("rows", "rep", None, None),
        P(),
        P(),
        P(("rows", "rep"), None),
    )
    out_specs = (P(("rows", "rep"), None), P(), P())
    return jax.shard_map(local, mesh=mesh, in_specs=in_specs, out_specs=out_specs, check_vma=False)
```

profile of v0, /device:TPU:0, one launch (start us, length us, event | category | flops | bytes accessed | tf_op | source)
XLA Modules:
  0.0 340.4 jit_solution(6113858609742054263)
XLA Ops:
  7.9 1.0 multiply_convert_fusion.1
  9.0 4.1 %collective-permute-start.1 = (bf16[512,128]{1,0:T(8,128)(2,1)S(1)}, bf16[512,128]{1,0:T(8,128)(2,1)S(1)}, u32[]{:S(2)}, u32[]{:S(2)}) collective-permute-start(bf16[512,128]{1,0:T(8,128)(2,1)S(1)} %multiply_convert_fusion.1), channel_id=1, source_target_pairs={{0,16},{2,18},{4,20},{6,22},{8,24},{10,26},{12,28},{14,30},{16,0},... | collective-permute-start | bytes 393224 | tf_op jit(solution)/shard_map/ppermute | solution.py:10
  14.5 0.8 broadcast_clamp_fusion.1
  15.3 0.8 fusion.21
  16.1 0.8 compare_and_fusion.1
  16.9 2.5 collective-permute-done.1
  19.4 1.0 broadcast_select_fusion.2
  20.4 12.1 %gather_fusion.1 = bf16[4096,128]{1,0:T(8,128)(2,1)S(1)} fusion(bf16[512,128]{1,0:T(8,128)(2,1)S(1)} %broadcast_select_fusion.2, s32[4096]{0:T(1024)S(1)} %broadcast_clamp_fusion.1), kind=kCustom, calls=%fused_computation.1.clone | custom fusion | bytes 2113536 | tf_op jit(solution)/shard_map/jit(_take)/gather | solution.py:24
  32.5 2.1 broadcast_select_fusion.1
  35.2 154.0 %while.19 = (s32[]{:T(128)}, bf16[512,128]{1,0:T(8,128)(2,1)S(1)}, f32[512,128]{1,0:T(8,128)S(1)}, s32[4,8,8]{2,1,0:T(8,128)}, s32[4,8,8,128]{3,2,1,0:T(8,128)},...) while((s32[]{:T(128)}, bf16[512,128]{1,0:T(8,128)(2,1)S(1)}, f32[512,128]{1,0:T(8,128)S(1)}, ...), condition=%wide.region_1.3_spmd, body=%wide.region_0.2_spmd.sunk | while | flops 135540768 | bytes 7202103 | solution.py:57
  35.2 4.2 %collective-permute-start = (bf16[512,128]{1,0:T(8,128)(2,1)S(1)}, bf16[512,128]{1,0:T(8,128)(2,1)S(1)}, u32[]{:S(2)}, u32[]{:S(2)}) collective-permute-start(bf16[512,128]{1,0:T(8,128)(2,1)S(1)} %get-tuple-element.281), channel_id=1, source_target_pairs={{0,30},{2,0},{4,2},{6,4},{8,6},{10,8},{12,10},{14,12},{16,14},{18,... | collective-permute-start | bytes 393224 | tf_op jit(solution)/shard_map/while/body/eval_jaxpr/ppermute | solution.py:10
  39.4 0.7 constant_dynamic-slice_fusion.3
  40.1 0.8 broadcast_clamp_fusion.3
  40.9 0.8 fusion.38
  41.7 0.8 compare_and_fusion.3
  42.5 12.1 %gather_fusion = bf16[4096,128]{1,0:T(8,128)(2,1)S(1)} fusion(bf16[512,128]{1,0:T(8,128)(2,1)S(1)} %collective-permute-done, s32[4096]{0:T(1024)S(1)} %broadcast_clamp_fusion.3), kind=kCustom, calls=%fused_computation.clone.clone.1 | custom fusion | bytes 2113536 | tf_op jit(solution)/shard_map/while/body/eval_jaxpr/jit(_take)/gather | solution.py:24
  54.6 2.1 broadcast_select_fusion.4
  57.3 4.0 %collective-permute-start = (bf16[512,128]{1,0:T(8,128)(2,1)S(1)}, bf16[512,128]{1,0:T(8,128)(2,1)S(1)}, u32[]{:S(2)}, u32[]{:S(2)}) collective-permute-start(bf16[512,128]{1,0:T(8,128)(2,1)S(1)} %get-tuple-element.281), channel_id=1, source_target_pairs={{0,30},{2,0},{4,2},{6,4},{8,6},{10,8},{12,10},{14,12},{16,14},{18,... | collective-permute-start | bytes 393224 | tf_op jit(solution)/shard_map/while/body/eval_jaxpr/ppermute | solution.py:10
  61.4 0.7 constant_dynamic-slice_fusion.3
  62.1 0.8 broadcast_clamp_fusion.3
  62.9 0.8 fusion.38
  63.7 0.8 compare_and_fusion.3
  64.5 12.1 %gather_fusion = bf16[4096,128]{1,0:T(8,128)(2,1)S(1)} fusion(bf16[512,128]{1,0:T(8,128)(2,1)S(1)} %collective-permute-done, s32[4096]{0:T(1024)S(1)} %broadcast_clamp_fusion.3), kind=kCustom, calls=%fused_computation.clone.clone.1 | custom fusion | bytes 2113536 | tf_op jit(solution)/shard_map/while/body/eval_jaxpr/jit(_take)/gather | solution.py:24
  76.7 2.1 broadcast_select_fusion.4
  79.3 4.0 %collective-permute-start = (bf16[512,128]{1,0:T(8,128)(2,1)S(1)}, bf16[512,128]{1,0:T(8,128)(2,1)S(1)}, u32[]{:S(2)}, u32[]{:S(2)}) collective-permute-start(bf16[512,128]{1,0:T(8,128)(2,1)S(1)} %get-tuple-element.281), channel_id=1, source_target_pairs={{0,30},{2,0},{4,2},{6,4},{8,6},{10,8},{12,10},{14,12},{16,14},{18,... | collective-permute-start | bytes 393224 | tf_op jit(solution)/shard_map/while/body/eval_jaxpr/ppermute | solution.py:10
  83.3 0.7 constant_dynamic-slice_fusion.3
  84.1 0.8 broadcast_clamp_fusion.3
  84.9 0.8 fusion.38
  85.7 0.8 compare_and_fusion.3
  86.5 12.1 %gather_fusion = bf16[4096,128]{1,0:T(8,128)(2,1)S(1)} fusion(bf16[512,128]{1,0:T(8,128)(2,1)S(1)} %collective-permute-done, s32[4096]{0:T(1024)S(1)} %broadcast_clamp_fusion.3), kind=kCustom, calls=%fused_computation.clone.clone.1 | custom fusion | bytes 2113536 | tf_op jit(solution)/shard_map/while/body/eval_jaxpr/jit(_take)/gather | solution.py:24
  98.6 2.1 broadcast_select_fusion.4
  101.3 4.0 %collective-permute-start = (bf16[512,128]{1,0:T(8,128)(2,1)S(1)}, bf16[512,128]{1,0:T(8,128)(2,1)S(1)}, u32[]{:S(2)}, u32[]{:S(2)}) collective-permute-start(bf16[512,128]{1,0:T(8,128)(2,1)S(1)} %get-tuple-element.281), channel_id=1, source_target_pairs={{0,30},{2,0},{4,2},{6,4},{8,6},{10,8},{12,10},{14,12},{16,14},{18,... | collective-permute-start | bytes 393224 | tf_op jit(solution)/shard_map/while/body/eval_jaxpr/ppermute | solution.py:10
  105.3 0.7 constant_dynamic-slice_fusion.3
  106.1 0.8 broadcast_clamp_fusion.3
  106.9 0.8 fusion.38
  107.6 0.8 compare_and_fusion.3
  108.4 12.1 %gather_fusion = bf16[4096,128]{1,0:T(8,128)(2,1)S(1)} fusion(bf16[512,128]{1,0:T(8,128)(2,1)S(1)} %collective-permute-done, s32[4096]{0:T(1024)S(1)} %broadcast_clamp_fusion.3), kind=kCustom, calls=%fused_computation.clone.clone.1 | custom fusion | bytes 2113536 | tf_op jit(solution)/shard_map/while/body/eval_jaxpr/jit(_take)/gather | solution.py:24
  120.6 2.1 broadcast_select_fusion.4
  123.3 4.0 %collective-permute-start = (bf16[512,128]{1,0:T(8,128)(2,1)S(1)}, bf16[512,128]{1,0:T(8,128)(2,1)S(1)}, u32[]{:S(2)}, u32[]{:S(2)}) collective-permute-start(bf16[512,128]{1,0:T(8,128)(2,1)S(1)} %get-tuple-element.281), channel_id=1, source_target_pairs={{0,30},{2,0},{4,2},{6,4},{8,6},{10,8},{12,10},{14,12},{16,14},{18,... | collective-permute-start | bytes 393224 | tf_op jit(solution)/shard_map/while/body/eval_jaxpr/ppermute | solution.py:10
  127.3 0.7 constant_dynamic-slice_fusion.3
  128.0 0.8 broadcast_clamp_fusion.3
  128.8 0.8 fusion.38
  129.6 0.8 compare_and_fusion.3
  130.4 12.1 %gather_fusion = bf16[4096,128]{1,0:T(8,128)(2,1)S(1)} fusion(bf16[512,128]{1,0:T(8,128)(2,1)S(1)} %collective-permute-done, s32[4096]{0:T(1024)S(1)} %broadcast_clamp_fusion.3), kind=kCustom, calls=%fused_computation.clone.clone.1 | custom fusion | bytes 2113536 | tf_op jit(solution)/shard_map/while/body/eval_jaxpr/jit(_take)/gather | solution.py:24
  142.6 2.1 broadcast_select_fusion.4
  145.3 4.0 %collective-permute-start = (bf16[512,128]{1,0:T(8,128)(2,1)S(1)}, bf16[512,128]{1,0:T(8,128)(2,1)S(1)}, u32[]{:S(2)}, u32[]{:S(2)}) collective-permute-start(bf16[512,128]{1,0:T(8,128)(2,1)S(1)} %get-tuple-element.281), channel_id=1, source_target_pairs={{0,30},{2,0},{4,2},{6,4},{8,6},{10,8},{12,10},{14,12},{16,14},{18,... | collective-permute-start | bytes 393224 | tf_op jit(solution)/shard_map/while/body/eval_jaxpr/ppermute | solution.py:10
  150.0 0.8 broadcast_clamp_fusion.3
  150.8 0.8 fusion.38
  151.6 0.8 compare_and_fusion.3
  152.4 12.1 %gather_fusion = bf16[4096,128]{1,0:T(8,128)(2,1)S(1)} fusion(bf16[512,128]{1,0:T(8,128)(2,1)S(1)} %collective-permute-done, s32[4096]{0:T(1024)S(1)} %broadcast_clamp_fusion.3), kind=kCustom, calls=%fused_computation.clone.clone.1 | custom fusion | bytes 2113536 | tf_op jit(solution)/shard_map/while/body/eval_jaxpr/jit(_take)/gather | solution.py:24
  164.5 2.1 broadcast_select_fusion.4
  167.2 4.0 %collective-permute-start = (bf16[512,128]{1,0:T(8,128)(2,1)S(1)}, bf16[512,128]{1,0:T(8,128)(2,1)S(1)}, u32[]{:S(2)}, u32[]{:S(2)}) collective-permute-start(bf16[512,128]{1,0:T(8,128)(2,1)S(1)} %get-tuple-element.281), channel_id=1, source_target_pairs={{0,30},{2,0},{4,2},{6,4},{8,6},{10,8},{12,10},{14,12},{16,14},{18,... | collective-permute-start | bytes 393224 | tf_op jit(solution)/shard_map/while/body/eval_jaxpr/ppermute | solution.py:10
  172.0 0.8 broadcast_clamp_fusion.3
  172.8 0.8 fusion.38
  173.6 0.8 compare_and_fusion.3
  174.4 12.1 %gather_fusion = bf16[4096,128]{1,0:T(8,128)(2,1)S(1)} fusion(bf16[512,128]{1,0:T(8,128)(2,1)S(1)} %collective-permute-done, s32[4096]{0:T(1024)S(1)} %broadcast_clamp_fusion.3), kind=kCustom, calls=%fused_computation.clone.clone.1 | custom fusion | bytes 2113536 | tf_op jit(solution)/shard_map/while/body/eval_jaxpr/jit(_take)/gather | solution.py:24
  186.5 2.1 broadcast_select_fusion.4
  190.1 12.4 %reduce-scatter.2.cloned.1.call-done = f32[256,128]{1,0:T(8,128)} async-done(((f32[512,128]{1,0:T(8,128)}), f32[256,128]{1,0:T(8,128)}) %reduce-scatter.2.cloned.1.call-update) | async-done | bytes 131088 | tf_op jit(solution)/shard_map/reduce_scatter | solution.py:58
  202.4 1.0 multiply_convert_fusion.2
  203.5 1.0 convert_reduce_fusion
  204.5 0.9 fusion.27
  205.4 39.4 %psum.15 = f32[256]{0:T(256)} all-reduce(f32[256]{0:T(256)S(1)} %get-tuple-element.225), channel_id=1, replica_groups=mesh['rows'=16,'rep'=2] {'rows','rep'}, use_global_device_ids=true, to_apply=%region_5.7 | all-reduce | flops 256 | bytes 2048 | tf_op jit(solution)/shard_map/psum | solution.py:71
  244.7 87.3 %all-reduce.2.cloned.1.call-done = f32[128,256]{1,0:T(8,128)} async-done(((f32[128,256]{1,0:T(8,128)}), f32[128,256]{1,0:T(8,128)}) %all-reduce.2.cloned.1.call-update) | async-done | bytes 131088 | tf_op jit(solution)/shard_map/psum | solution.py:71
  332.0 1.6 copy.29
  (54 shorter events, 8.6 us)
Async XLA Ops:
  7.2 196.3 %copy-start = (bf16[128,256]{1,0:T(8,128)(2,1)S(1)}, bf16[128,256]{1,0:T(8,128)(2,1)}, u32[]{:S(2)}) copy-start(bf16[128,256]{1,0:T(8,128)(2,1)} %param.17) | copy-start | bytes 196612
  7.2 195.3 %reduce-scatter.2.cloned.1.call-start = ((), (), s32[]{:S(2)}) async-start(), calls=%async_computation.1 | async-start | bytes 393216 | tf_op jit(solution)/shard_map/reduce_scatter | solution.py:58
  9.0 10.4 %collective-permute-start.1 = (bf16[512,128]{1,0:T(8,128)(2,1)S(1)}, bf16[512,128]{1,0:T(8,128)(2,1)S(1)}, u32[]{:S(2)}, u32[]{:S(2)}) collective-permute-start(bf16[512,128]{1,0:T(8,128)(2,1)S(1)} %multiply_convert_fusion.1), channel_id=1, source_target_pairs={{0,16},{2,18},{4,20},{6,22},{8,24},{10,26},{12,28},{14,30},{16,0},... | collective-permute-start | bytes 393224 | tf_op jit(solution)/shard_map/ppermute | solution.py:10
  35.2 168.3 %copy-start.2 = (bf16[256,256]{1,0:T(8,128)(2,1)S(1)}, bf16[256,256]{1,0:T(8,128)(2,1)}, u32[]{:S(2)}) copy-start(bf16[256,256]{1,0:T(8,128)(2,1)} %param.19) | copy-start | bytes 393220
  35.2 168.3 %copy-start.3 = (f32[256]{0:T(256)S(1)}, f32[256]{0:T(256)}, u32[]{:S(2)}) copy-start(f32[256]{0:T(256)} %param.18) | copy-start | bytes 3076
  35.2 7.3 %collective-permute-start = (bf16[512,128]{1,0:T(8,128)(2,1)S(1)}, bf16[512,128]{1,0:T(8,128)(2,1)S(1)}, u32[]{:S(2)}, u32[]{:S(2)}) collective-permute-start(bf16[512,128]{1,0:T(8,128)(2,1)S(1)} %get-tuple-element.281), channel_id=1, source_target_pairs={{0,30},{2,0},{4,2},{6,4},{8,6},{10,8},{12,10},{14,12},{16,14},{18,... | collective-permute-start | bytes 393224 | tf_op jit(solution)/shard_map/while/body/eval_jaxpr/ppermute | solution.py:10
  57.3 7.2 %collective-permute-start = (bf16[512,128]{1,0:T(8,128)(2,1)S(1)}, bf16[512,128]{1,0:T(8,128)(2,1)S(1)}, u32[]{:S(2)}, u32[]{:S(2)}) collective-permute-start(bf16[512,128]{1,0:T(8,128)(2,1)S(1)} %get-tuple-element.281), channel_id=1, source_target_pairs={{0,30},{2,0},{4,2},{6,4},{8,6},{10,8},{12,10},{14,12},{16,14},{18,... | collective-permute-start | bytes 393224 | tf_op jit(solution)/shard_map/while/body/eval_jaxpr/ppermute | solution.py:10
  79.3 7.1 %collective-permute-start = (bf16[512,128]{1,0:T(8,128)(2,1)S(1)}, bf16[512,128]{1,0:T(8,128)(2,1)S(1)}, u32[]{:S(2)}, u32[]{:S(2)}) collective-permute-start(bf16[512,128]{1,0:T(8,128)(2,1)S(1)} %get-tuple-element.281), channel_id=1, source_target_pairs={{0,30},{2,0},{4,2},{6,4},{8,6},{10,8},{12,10},{14,12},{16,14},{18,... | collective-permute-start | bytes 393224 | tf_op jit(solution)/shard_map/while/body/eval_jaxpr/ppermute | solution.py:10
  101.3 7.1 %collective-permute-start = (bf16[512,128]{1,0:T(8,128)(2,1)S(1)}, bf16[512,128]{1,0:T(8,128)(2,1)S(1)}, u32[]{:S(2)}, u32[]{:S(2)}) collective-permute-start(bf16[512,128]{1,0:T(8,128)(2,1)S(1)} %get-tuple-element.281), channel_id=1, source_target_pairs={{0,30},{2,0},{4,2},{6,4},{8,6},{10,8},{12,10},{14,12},{16,14},{18,... | collective-permute-start | bytes 393224 | tf_op jit(solution)/shard_map/while/body/eval_jaxpr/ppermute | solution.py:10
  123.3 7.1 %collective-permute-start = (bf16[512,128]{1,0:T(8,128)(2,1)S(1)}, bf16[512,128]{1,0:T(8,128)(2,1)S(1)}, u32[]{:S(2)}, u32[]{:S(2)}) collective-permute-start(bf16[512,128]{1,0:T(8,128)(2,1)S(1)} %get-tuple-element.281), channel_id=1, source_target_pairs={{0,30},{2,0},{4,2},{6,4},{8,6},{10,8},{12,10},{14,12},{16,14},{18,... | collective-permute-start | bytes 393224 | tf_op jit(solution)/shard_map/while/body/eval_jaxpr/ppermute | solution.py:10
  145.3 7.1 %collective-permute-start = (bf16[512,128]{1,0:T(8,128)(2,1)S(1)}, bf16[512,128]{1,0:T(8,128)(2,1)S(1)}, u32[]{:S(2)}, u32[]{:S(2)}) collective-permute-start(bf16[512,128]{1,0:T(8,128)(2,1)S(1)} %get-tuple-element.281), channel_id=1, source_target_pairs={{0,30},{2,0},{4,2},{6,4},{8,6},{10,8},{12,10},{14,12},{16,14},{18,... | collective-permute-start | bytes 393224 | tf_op jit(solution)/shard_map/while/body/eval_jaxpr/ppermute | solution.py:10
  167.2 7.1 %collective-permute-start = (bf16[512,128]{1,0:T(8,128)(2,1)S(1)}, bf16[512,128]{1,0:T(8,128)(2,1)S(1)}, u32[]{:S(2)}, u32[]{:S(2)}) collective-permute-start(bf16[512,128]{1,0:T(8,128)(2,1)S(1)} %get-tuple-element.281), channel_id=1, source_target_pairs={{0,30},{2,0},{4,2},{6,4},{8,6},{10,8},{12,10},{14,12},{16,14},{18,... | collective-permute-start | bytes 393224 | tf_op jit(solution)/shard_map/while/body/eval_jaxpr/ppermute | solution.py:10
  189.2 0.7 copy-start.1
  189.9 142.1 %all-reduce.2.cloned.1.call-start = ((), (), s32[]{:S(2)}) async-start(), calls=%async_computation.2 | async-start | bytes 262144 | tf_op jit(solution)/shard_map/psum | solution.py:71
Sparse Core Ops, SparseCore 0:
  190.0 12.3 reduce-scatter.1
  209.5 122.4 all-reduce.1
where the time goes:
time: 342 us; the launch traced here: 340 us
  local copies, waits for them, and re-layouts  105 us (31%)
  waiting for transfers between devices  102 us (30%)
  other arithmetic  41.1 us (12%)
  blocking collectives  39.4 us (12%)
  starting transfers between devices  32.3 us (9%)
  between operations  14.1 us (4%)
  matrix products  5.53 us (2%)
    gather x8, local copies, waits for them, and re-layouts, tile_sums(): jnp.take(buffer, far_node.reshape(-1), axis=0)  97.1 us
    psum x1, waiting for transfers between devices, local(): lax.psum((local_weight, local_bias), ('rows', 'rep'))  87.3 us
    psum x1, blocking collectives, local(): lax.psum((local_weight, local_bias), ('rows', 'rep'))  39.4 us
    ppermute x8, starting transfers between devices, from_behind(): return lax.ppermute(value, axis, pairs)  32.2 us
    select_n x8, other arithmetic, tile_sums(): jnp.take(buffer, far_node.reshape(-1), axis=0)  17.2 us
    reduce_scatter x1, waiting for transfers between devices, local(): lax.psum_scatter(partial_total, 'rep', scatter_dimension=0, tiled=True)  12.4 us
  transfers between devices with their start and end apart: 10, of which 3 were waited for; matrix products, arithmetic and copies ran while one was open for 8% of the time, Pallas kernels for 0%

commit v1 on v0

v1 whole, which is shorter than its diff:
```python
import functools

import jax
import jax.numpy as jnp
from jax import lax
from jax.experimental import pallas as pl
from jax.experimental.pallas import tpu as pltpu
from jax.sharding import PartitionSpec as P

MESH = pl.DeviceIdType.MESH
BLK = 128
GELU_C = 0.7978845608028654
GELU_A = 0.044715


def kernel(
    n_rows, n_rep, fuse_sum,
    feat_ref, deg_ref, tb_ref, cnt_ref, code_ref, w_ref, b_ref, cot_ref,
    act_ref, gw_ref, gb_ref,
    own, flat, invb, adj, gathered, part, precv, gwp, grecv, gfin,
    s_send, s_recv, p_send, p_recv, g_send, g_recv, f_send, f_recv,
):
    blocks, steps, slots, ecap = code_ref.shape
    nodes = blocks * BLK
    n_dev = n_rows * n_rep
    row = lax.axis_index("rows")
    rep = lax.axis_index("rep")
    me = row * n_rep + rep
    share = nodes // n_rep

    barrier = pltpu.get_barrier_semaphore()
    if fuse_sum:
        @pl.loop(1, n_dev)
        def _(d):
            p = lax.rem(me + d, n_dev)
            pl.semaphore_signal(
                barrier, inc=1, device_id=(p // n_rep, lax.rem(p, n_rep)), device_id_type=MESH
            )
    else:
        for j in range(steps):
            off = rep * steps + j

            def greet(off=off):
                pl.semaphore_signal(
                    barrier, inc=1, device_id=(lax.rem(row + off, n_rows), rep), device_id_type=MESH
                )

            if j == 0:
                pl.when(off != 0)(greet)
            else:
                greet()
        for d in range(1, n_rep):
            pl.semaphore_signal(
                barrier, inc=1, device_id=(row, lax.rem(rep + d, n_rep)), device_id_type=MESH
            )

    inv = lax.rsqrt(deg_ref[...].astype(jnp.float32))
    inv_cols = jnp.concatenate([inv, jnp.zeros((8 - blocks, BLK), jnp.float32)], axis=0).T
    for i in range(blocks):
        rows = slice(i * BLK, (i + 1) * BLK)
        wide = jnp.broadcast_to(inv_cols[:, i : i + 1], (BLK, BLK))
        invb[rows, :] = wide
        scaled = (feat_ref[rows, :].astype(jnp.float32) * wide).astype(jnp.bfloat16)
        own[i] = scaled
        flat[rows, :] = scaled

    if fuse_sum:
        pl.semaphore_wait(barrier, n_dev - 1)
    else:
        pl.semaphore_wait(barrier, steps - 1 + n_rep - 1)

        @pl.when(rep != 0)
        def _():
            pl.semaphore_wait(barrier, 1)

    def send_of(j):
        off = rep * steps + j
        return pltpu.make_async_remote_copy(
            src_ref=own,
            dst_ref=gathered.at[pl.ds(j * blocks, blocks)],
            send_sem=s_send.at[j],
            recv_sem=s_recv.at[j],
            device_id=(lax.rem(row + n_rows - off, n_rows), rep),
            device_id_type=MESH,
        )

    for j in range(steps - 1, 0, -1):
        send_of(j).start()

    @pl.when(rep != 0)
    def _():
        send_of(0).start()

    @pl.when(rep == 0)
    def _():
        gathered[0:blocks] = own[...]

    sub = lax.broadcasted_iota(jnp.int32, (BLK, ecap), 0)
    lane = lax.broadcasted_iota(jnp.int32, (1, ecap), 1)
    one = jnp.ones((), jnp.float32)
    zero = jnp.zeros((), jnp.float32)

    @pl.loop(0, blocks * steps)
    def _(t):
        i = t // steps
        o = lax.rem(t, steps)
        codes = code_ref[i, o]
        for k in range(slots):
            code = codes[k : k + 1, :]
            target = jnp.where(lane < cnt_ref[i, o, k], code >> 7, -1)
            far = code & (BLK - 1)
            hot_t = jnp.where(sub == target, one, zero).astype(jnp.bfloat16)
            hot_c = jnp.where(sub == far, one, zero).astype(jnp.bfloat16)
            tile = lax.dot_general(
                hot_t, hot_c, (((1,), (1,)), ((), ())), preferred_element_type=jnp.float32
            )
            adj[t, :, k * BLK : (k + 1) * BLK] = tile.astype(jnp.bfloat16)

    for j in range(steps - 1, 0, -1):
        send_of(j).wait()

    @pl.when(rep != 0)
    def _():
        send_of(0).wait()

    whole_blocks = share // BLK if share % BLK == 0 else 0
    first = blocks - whole_blocks
    start_block = lax.rem((rep + 1) * whole_blocks, blocks)

    def sum_block(s):
        i = lax.rem(start_block + s, blocks)

        def body(o, acc):
            picked = jnp.concatenate(
                [
                    gathered[o * blocks + tb_ref[i, o, k]]
                    for k in range(slots)
                ],
                axis=0,
            )
            return acc + jnp.dot(adj[i * steps + o], picked, preferred_element_type=jnp.float32)

        total = lax.fori_loop(0, steps, body, jnp.zeros((BLK, BLK), jnp.float32))
        part[pl.ds(pl.multiple_of(i * BLK, BLK), BLK), :] = total

    @pl.loop(0, first)
    def _(s):
        sum_block(s)

    def part_of(d):
        peer = lax.rem(rep + d, n_rep)
        return pltpu.make_async_remote_copy(
            src_ref=part.at[pl.ds(pl.multiple_of(peer * share, share), share)],
            dst_ref=precv.at[d - 1],
            send_sem=p_send.at[d - 1],
            recv_sem=p_recv.at[d - 1],
            device_id=(row, peer),
            device_id_type=MESH,
        )

    for d in range(1, n_rep):
        part_of(d).start()

    if first < blocks:
        @pl.loop(first, blocks)
        def _(s):
            sum_block(s)

    mine = pl.ds(pl.multiple_of(rep * share, share), share)
    sums = part[mine, :] + flat[mine, :].astype(jnp.float32)
    for d in range(1, n_rep):
        part_of(d).wait()
        sums = sums + precv[d - 1]
    aggregate = (invb[mine, :] * sums).astype(jnp.bfloat16)
    x = jnp.dot(aggregate, w_ref[...], preferred_element_type=jnp.float32) + b_ref[...]
    x2 = x * x
    t = jnp.tanh(GELU_C * (x + GELU_A * (x2 * x)))
    cdf = 0.5 * (1.0 + t)
    act_ref[...] = (x * cdf).astype(jnp.bfloat16)
    slope = cdf + x * (0.5 * (1.0 - t * t)) * (GELU_C * (1.0 + (3.0 * GELU_A) * x2))
    delta = (cot_ref[...].astype(jnp.float32) * slope).astype(jnp.bfloat16)
    bias_sum = jnp.sum(delta.astype(jnp.float32), axis=0, keepdims=True)
    weight_sum = lax.dot_general(
        aggregate, delta, (((0,), (0,)), ((), ())), preferred_element_type=jnp.float32
    )
    if not fuse_sum:
        gw_ref[...] = weight_sum
        gb_ref[...] = bias_sum
        return

    halves = weight_sum.shape[1] // BLK
    for p in range(n_dev):
        r0, c0 = p // halves * 8, p % halves * BLK
        gwp[p, 0:8, :] = weight_sum[r0 : r0 + 8, c0 : c0 + BLK]
        gwp[p, 8:9, :] = bias_sum[:, c0 : c0 + BLK]

    @pl.loop(1, n_dev)
    def _(d):
        p = lax.rem(me + d, n_dev)
        pltpu.make_async_remote_copy(
            src_ref=gwp.at[p],
            dst_ref=grecv.at[me],
            send_sem=g_send,
            recv_sem=g_recv,
            device_id=(p // n_rep, lax.rem(p, n_rep)),
            device_id_type=MESH,
        ).start()

    others = pl.ds(0, n_dev - 1)

    def all_of(src, dst, send_sem, recv_sem):
        p = lax.rem(me + 1, n_dev)
        return pltpu.make_async_remote_copy(
            src_ref=src.at[others],
            dst_ref=dst.at[others],
            send_sem=send_sem,
            recv_sem=recv_sem,
            device_id=(p // n_rep, lax.rem(p, n_rep)),
            device_id_type=MESH,
        )

    grecv[me] = gwp[me]
    all_of(gwp, grecv, g_send, g_recv).wait_recv()
    total = grecv[0]
    for s in range(1, n_dev):
        total = total + grecv[s]
    gfin[me] = total

    @pl.loop(1, n_dev)
    def _(d):
        p = lax.rem(me + d, n_dev)
        pltpu.make_async_remote_copy(
            src_ref=gfin.at[me],
            dst_ref=gfin.at[me],
            send_sem=f_send,
            recv_sem=f_recv,
            device_id=(p // n_rep, lax.rem(p, n_rep)),
            device_id_type=MESH,
        ).start()

    all_of(gwp, grecv, g_send, g_recv).wait_send()
    all_of(gfin, gfin, f_send, f_recv).wait_recv()
    for p in range(n_dev):
        r0, c0 = p // halves * 8, p % halves * BLK
        gw_ref[r0 : r0 + 8, c0 : c0 + BLK] = gfin[p, 0:8, :]
    for h in range(halves):
        gb_ref[:, h * BLK : (h + 1) * BLK] = gfin[h, 8:9, :]
    all_of(gfin, gfin, f_send, f_recv).wait_send()


def local(features, degree, tile_block, edge_count, edge_code, weight, bias, cotangent):
    n_rows = lax.axis_size("rows")
    n_rep = lax.axis_size("rep")
    n_dev = n_rows * n_rep
    blocks, steps, slots, ecap = edge_code.shape
    nodes, feat = features.shape
    hidden = weight.shape[1]
    share = nodes // n_rep
    fuse_sum = feat * hidden == n_dev * 8 * BLK
    held = n_dev if fuse_sum else 1
    vmem = pl.BlockSpec(memory_space=pltpu.VMEM)
    smem = pl.BlockSpec(memory_space=pltpu.SMEM)
    dma = pltpu.SemaphoreType.DMA
    others = max(n_rep - 1, 1)
    act, grad_w, grad_b = pl.pallas_call(
        functools.partial(kernel, n_rows, n_rep, fuse_sum),
        out_shape=(
            jax.ShapeDtypeStruct((share, hidden), jnp.bfloat16),
            jax.ShapeDtypeStruct((feat, hidden), jnp.float32),
            jax.ShapeDtypeStruct((1, hidden), jnp.float32),
        ),
        in_specs=[vmem, vmem, smem, smem, vmem, vmem, vmem, vmem],
        out_specs=(vmem, vmem, vmem),
        scratch_shapes=[
            pltpu.VMEM((blocks, BLK, feat), jnp.bfloat16),
            pltpu.VMEM((nodes, feat), jnp.bfloat16),
            pltpu.VMEM((nodes, feat), jnp.float32),
            pltpu.VMEM((blocks * steps, BLK, slots * BLK), jnp.bfloat16),
            pltpu.VMEM((steps * blocks, BLK, feat), jnp.bfloat16),
            pltpu.VMEM((nodes, feat), jnp.float32),
            pltpu.VMEM((others, share, feat), jnp.float32),
            pltpu.VMEM((held, 9, BLK), jnp.float32),
            pltpu.VMEM((held, 9, BLK), jnp.float32),
            pltpu.VMEM((held, 9, BLK), jnp.float32),
            dma((steps,)),
            dma((steps,)),
            dma((others,)),
            dma((others,)),
            dma(()),
            dma(()),
            dma(()),
            dma(()),
        ],
        compiler_params=pltpu.CompilerParams(
            collective_id=0, has_side_effects=True, vmem_limit_bytes=40 * 1024 * 1024
        ),
    )(
        features,
        degree.reshape(blocks, BLK),
        tile_block,
        edge_count,
        edge_code,
        weight,
        bias.reshape(1, hidden),
        cotangent,
    )
    grad_b = grad_b.reshape(hidden)
    if not fuse_sum:
        grad_w, grad_b = lax.psum((grad_w, grad_b), ("rows", "rep"))
    return (act, grad_w, grad_b)


def solution(mesh):
    in_specs = (
        P("rows", None),
        P("rows"),
        P("rows", "rep", None),
        P("rows", "rep", None),
        P("rows", "rep", None, None),
        P(),
        P(),
        P(("rows", "rep"), None),
    )
    out_specs = (P(("rows", "rep"), None), P(), P())
    return jax.shard_map(local, mesh=mesh, in_specs=in_specs, out_specs=out_specs, check_vma=False)
```

time: 342 us -> 67.4 us (0.20)
  waiting for transfers between devices: 102 us -> 0 us
  local copies, waits for them, and re-layouts: 105 us -> 7.54 us
  Pallas kernels: 0 us -> 58.8 us
  other arithmetic: 41.1 us -> 0 us
  blocking collectives: 39.4 us -> 0 us
  starting transfers between devices: 32.3 us -> 0 us
  between operations: 14.1 us -> 0.67 us
  matrix products: 5.53 us -> 0 us
    gather x8 -> x0, local copies, waits for them, and re-layouts: 97.1 us -> none  [tile_sums(): jnp.take(buffer, far_node.reshape(-1), axis=0)]
    psum x1 -> x0, waiting for transfers between devices: 87.3 us -> none  [local(): lax.psum((local_weight, local_bias), ('rows', 'rep'))]
    pallas_call x0 -> x1, Pallas kernels: none -> 58.8 us  [local(): pl.pallas_call(functools.partial(kernel, n_rows, n_rep, fuse_sum), out_sh...]
    psum x1 -> x0, blocking collectives: 39.4 us -> none  [local(): lax.psum((local_weight, local_bias), ('rows', 'rep'))]
    ppermute x8 -> x0, starting transfers between devices: 32.2 us -> none  [from_behind(): return lax.ppermute(value, axis, pairs)]
    select_n x17 -> x0, other arithmetic: 24.5 us -> none  [the longest x8 17.2 us: tile_sums(): jnp.take(buffer, far_node.reshape(-1), axis=0)]
    reduce_scatter x1 -> x0, waiting for transfers between devices: 12.4 us -> none  [local(): lax.psum_scatter(partial_total, 'rep', scatter_dimension=0, tiled=True)]
    gather x8 -> x0, other arithmetic: 6.4 us -> none
  transfers between devices with their start and end apart: 10 -> 0, of which waited for: 3 -> 0; matrix products, arithmetic and copies ran while one was open for 8% -> 0% of each run, Pallas kernels for 0% -> 0%
where the time goes in v1:
time: 67.4 us; the launch traced here: 67 us
  Pallas kernels  58.8 us (87%)
  local copies, waits for them, and re-layouts  7.54 us (11%)
    pallas_call x1, Pallas kernels, local(): pl.pallas_call(functools.partial(kernel, n_rows, n_rep, fuse_sum), out_sh...  58.8 us
    unnamed x19, local copies, waits for them, and re-layouts  7.54 us

profile of v1, /device:TPU:0, one launch (start us, length us, event | category | flops | bytes accessed | tf_op | source)
XLA Modules:
  0.0 67.0 jit_solution(15331045765997568312)
XLA Ops:
  0.6 0.0 copy-start.6
  0.6 0.0 copy-start.7
  0.7 0.7 copy-done.6
  1.3 0.0 copy-done.7
  1.3 0.0 copy-start
  1.3 0.9 %copy-done = bf16[512,128]{1,0:T(8,128)(2,1)S(1)} copy-done((bf16[512,128]{1,0:T(8,128)(2,1)S(1)}, bf16[512,128]{1,0:T(8,128)(2,1)}, u32[]{:S(2)}) %copy-start) | copy-done | bytes 131096
  2.2 0.0 copy-start.1
  2.2 0.9 %copy-done.1 = s32[4,8,8,128]{3,2,1,0:T(8,128)S(1)} copy-done((s32[4,8,8,128]{3,2,1,0:T(8,128)S(1)}, s32[4,8,8,128]{3,2,1,0:T(8,128)}, u32[]{:S(2)}) %copy-start.1) | copy-done | bytes 131096
  3.1 0.0 copy-start.2
  3.1 0.9 %copy-done.2 = bf16[256,256]{1,0:T(8,128)(2,1)S(1)} copy-done((bf16[256,256]{1,0:T(8,128)(2,1)S(1)}, bf16[256,256]{1,0:T(8,128)(2,1)}, u32[]{:S(2)}) %copy-start.2) | copy-done | bytes 131096
  4.0 0.0 copy-start.3
  4.0 0.8 %copy-done.3 = bf16[128,256]{1,0:T(8,128)(2,1)S(1)} copy-done((bf16[128,256]{1,0:T(8,128)(2,1)S(1)}, bf16[128,256]{1,0:T(8,128)(2,1)}, u32[]{:S(2)}) %copy-start.3) | copy-done | bytes 65560
  4.9 0.0 copy-start.4
  4.9 0.7 %copy-done.4 = s32[4,8,8]{2,1,0:T(8,128)S(1)} copy-done((s32[4,8,8]{2,1,0:T(8,128)S(1)}, s32[4,8,8]{2,1,0:T(8,128)}, u32[]{:S(2)}) %copy-start.4) | copy-done | bytes 1048
  5.6 0.0 copy-start.5
  5.6 0.7 %copy-done.5 = s32[4,8,8]{2,1,0:T(8,128)S(1)} copy-done((s32[4,8,8]{2,1,0:T(8,128)S(1)}, s32[4,8,8]{2,1,0:T(8,128)}, u32[]{:S(2)}) %copy-start.5) | copy-done | bytes 1048
  6.3 58.8 %shard_map.103 = (bf16[256,256]{1,0:T(8,128)(2,1)S(1)}, f32[128,256]{1,0:T(8,128)S(1)}, f32[1,256]{1,0:T(1,128)S(1)}) custom-call(bf16[512,128]{1,0:T(8,128)(2,1)S(1)} %copy-done, s32[4,128]{1,0:T(4,128)S(1)} %bitcast.3, s32[4,8,8]{2,1,0:T(8,128)S(1)} %copy-done.4, s32[4,8,8]{2,1,0:T(8,128)S(1)} %copy-done.5, s32[4,8,8,128]{3,2,1,0:T(8,128)S(1)} %copy-done.1, ...), custom_call_target="tpu_custom_call" | custom-call | tf_op jit(solution)/shard_map/pallas_call | solution.py:265
  65.2 0.7 copy.14
  65.8 0.7 copy.15
  66.5 0.6 copy.16
Async XLA Ops:
  0.6 0.7 %copy-start.6 = (s32[512]{0:T(512)S(1)}, s32[512]{0:T(512)}, u32[]{:S(2)}) copy-start(s32[512]{0:T(512)} %param.9) | copy-start | bytes 6148
  0.6 0.7 %copy-start.7 = (f32[256]{0:T(256)S(1)}, f32[256]{0:T(256)}, u32[]{:S(2)}) copy-start(f32[256]{0:T(256)} %param.14) | copy-start | bytes 3076
  1.3 0.9 %copy-start = (bf16[512,128]{1,0:T(8,128)(2,1)S(1)}, bf16[512,128]{1,0:T(8,128)(2,1)}, u32[]{:S(2)}) copy-start(bf16[512,128]{1,0:T(8,128)(2,1)} %feat_ref.1) | copy-start | bytes 393220
  2.2 0.9 %copy-start.1 = (s32[4,8,8,128]{3,2,1,0:T(8,128)S(1)}, s32[4,8,8,128]{3,2,1,0:T(8,128)}, u32[]{:S(2)}) copy-start(s32[4,8,8,128]{3,2,1,0:T(8,128)} %code_ref.1) | copy-start | bytes 393220
  3.1 0.9 %copy-start.2 = (bf16[256,256]{1,0:T(8,128)(2,1)S(1)}, bf16[256,256]{1,0:T(8,128)(2,1)}, u32[]{:S(2)}) copy-start(bf16[256,256]{1,0:T(8,128)(2,1)} %cot_ref.1) | copy-start | bytes 393220
  4.0 0.8 %copy-start.3 = (bf16[128,256]{1,0:T(8,128)(2,1)S(1)}, bf16[128,256]{1,0:T(8,128)(2,1)}, u32[]{:S(2)}) copy-start(bf16[128,256]{1,0:T(8,128)(2,1)} %w_ref.1) | copy-start | bytes 196612
  4.9 0.7 %copy-start.4 = (s32[4,8,8]{2,1,0:T(8,128)S(1)}, s32[4,8,8]{2,1,0:T(8,128)}, u32[]{:S(2)}) copy-start(s32[4,8,8]{2,1,0:T(8,128)} %tb_ref.1) | copy-start | bytes 3076
  5.6 0.7 %copy-start.5 = (s32[4,8,8]{2,1,0:T(8,128)S(1)}, s32[4,8,8]{2,1,0:T(8,128)}, u32[]{:S(2)}) copy-start(s32[4,8,8]{2,1,0:T(8,128)} %cnt_ref.1) | copy-start | bytes 3076

commit v2 on v1

v2 whole, which is shorter than its diff:
```python
import functools

import jax
import jax.numpy as jnp
from jax import lax
from jax.experimental import pallas as pl
from jax.experimental.pallas import tpu as pltpu
from jax.sharding import PartitionSpec as P

MESH = pl.DeviceIdType.MESH
BLK = 128
GELU_C = 0.7978845608028654
GELU_A = 0.044715


def kernel(
    n_rows, n_rep, fuse_sum,
    feat_hbm, deg_hbm, tb_hbm, cnt_hbm, code_hbm, w_hbm, b_hbm, cot_hbm,
    act_ref, gw_ref, gb_ref,
    feat_ref, deg_ref, tb_ref, cnt_ref, code_ref, w_ref, b_ref, cot_ref,
    own, invb, adj, gathered, part, precv, gwp, grecv, gfin,
    in_sem, d_send, f_send, s_recv, p_send, p_recv, g_send, g_recv, o_send, o_recv,
):
    blocks, steps, slots, ecap = code_ref.shape
    nodes = blocks * BLK
    n_dev = n_rows * n_rep
    row = lax.axis_index("rows")
    rep = lax.axis_index("rep")
    core = lax.rem(row, 2)
    sibling = row + 1 - 2 * core
    me = row * n_rep + rep
    share = nodes // n_rep
    base = rep * steps

    def load(n, src, dst):
        return pltpu.make_async_copy(src, dst, in_sem.at[n])

    loads = [
        load(n, src, dst)
        for n, (src, dst) in enumerate(
            (
                (deg_hbm, deg_ref),
                (feat_hbm, feat_ref),
                (code_hbm, code_ref),
                (tb_hbm, tb_ref),
                (cnt_hbm, cnt_ref),
                (w_hbm, w_ref),
                (b_hbm, b_ref),
                (cot_hbm, cot_ref),
            )
        )
    ]
    for copy in loads:
        copy.start()

    barrier = pltpu.get_barrier_semaphore()

    def greet(to_row, to_rep):
        pl.semaphore_signal(barrier, inc=1, device_id=(to_row, to_rep), device_id_type=MESH)

    if fuse_sum:
        @pl.loop(1, n_dev)
        def _(d):
            p = lax.rem(me + d, n_dev)
            greet(p // n_rep, lax.rem(p, n_rep))
    else:
        for e in range(2, steps, 2):
            greet(lax.rem(row + base + e, n_rows), rep)

        @pl.when(rep != 0)
        def _():
            greet(lax.rem(row + base, n_rows), rep)

        greet(sibling, rep)

        @pl.when(core == 1)
        def _():
            greet(lax.rem(row + base + steps - 1, n_rows), rep)

        for d in range(1, n_rep):
            greet(row, lax.rem(rep + d, n_rep))

    loads[0].wait()
    inv = lax.rsqrt(deg_ref[...].astype(jnp.float32))
    inv_cols = jnp.concatenate([inv, jnp.zeros((8 - blocks, BLK), jnp.float32)], axis=0).T
    loads[1].wait()
    for i in range(blocks):
        rows = slice(i * BLK, (i + 1) * BLK)
        wide = jnp.broadcast_to(inv_cols[:, i : i + 1], (BLK, BLK))
        invb[rows, :] = wide
        own[rows, :] = (feat_ref[rows, :].astype(jnp.float32) * wide).astype(jnp.bfloat16)

    if fuse_sum:
        pl.semaphore_wait(barrier, n_dev - 1)
    else:
        pl.semaphore_wait(barrier, steps // 2 - 1 + 1 + n_rep - 1)

        @pl.when(rep != 0)
        def _():
            pl.semaphore_wait(barrier, 1)

        @pl.when(core == 0)
        def _():
            pl.semaphore_wait(barrier, 1)

    def direct(e):
        return pltpu.make_async_remote_copy(
            src_ref=own,
            dst_ref=gathered.at[e],
            send_sem=d_send.at[e // 2],
            recv_sem=s_recv.at[e],
            device_id=(lax.rem(row + n_rows - base - e, n_rows), rep),
            device_id_type=MESH,
        )

    def across():
        return pltpu.make_async_remote_copy(
            src_ref=own,
            dst_ref=gathered.at[steps - 1],
            send_sem=d_send.at[steps // 2],
            recv_sem=s_recv.at[steps - 1],
            device_id=(lax.rem(row + n_rows - base - steps + 1, n_rows), rep),
            device_id_type=MESH,
        )

    def pass_on(e):
        slot = e - 1 + 2 * core
        return pltpu.make_async_remote_copy(
            src_ref=gathered.at[e],
            dst_ref=gathered.at[slot],
            send_sem=f_send.at[e // 2],
            recv_sem=s_recv.at[slot],
            device_id=(sibling, rep),
            device_id_type=MESH,
        )

    def arrival(slot):
        return pltpu.make_async_remote_copy(
            src_ref=own,
            dst_ref=gathered.at[slot],
            send_sem=d_send.at[0],
            recv_sem=s_recv.at[slot],
            device_id=(sibling, rep),
            device_id_type=MESH,
        )

    @pl.when(rep != 0)
    def _():
        direct(0).start()

    for e in range(2, steps, 2):
        direct(e).start()

    @pl.when(core == 0)
    def _():
        across().start()

    @pl.when(rep == 0)
    def _():
        gathered[0] = own[...]

    sub = lax.broadcasted_iota(jnp.int32, (BLK, ecap), 0).astype(jnp.float32).astype(jnp.bfloat16)
    lane = lax.broadcasted_iota(jnp.int32, (1, ecap), 1)
    one = jnp.ones((BLK, ecap), jnp.bfloat16)
    zero = jnp.zeros((BLK, ecap), jnp.bfloat16)
    for copy in loads[2:5]:
        copy.wait()

    def hot(index):
        index = jnp.broadcast_to(index.astype(jnp.float32), (BLK, ecap)).astype(jnp.bfloat16)
        return jnp.where(sub == index, one, zero)

    def build(t):
        i = t // steps
        o = lax.rem(t, steps)
        codes = code_ref[i, o]
        targets, fars = [], []
        for k in range(slots):
            code = codes[k : k + 1, :]
            far = code & (BLK - 1)
            targets.append(hot(jnp.where(lane < cnt_ref[i, o, k], code >> 7, -1)))
            fars.append(
                jnp.concatenate(
                    [hot(jnp.where(tb_ref[i, o, k] == q, far, -1)) for q in range(blocks)], axis=0
                )
            )
        tile = lax.dot_general(
            jnp.concatenate(targets, axis=1),
            jnp.concatenate(fars, axis=1),
            (((1,), (1,)), ((), ())),
            preferred_element_type=jnp.float32,
        )
        adj[o, pl.ds(pl.multiple_of(i * BLK, BLK), BLK), :] = tile.astype(jnp.bfloat16)

    chunk = blocks * steps // (steps // 2)
    for e in range(0, steps, 2):
        @pl.loop(e // 2 * chunk, (e // 2 + 1) * chunk)
        def _(t):
            build(t)

        if e == 0:
            @pl.when(rep != 0)
            def _():
                direct(0).wait_recv()

            @pl.when(core == 1)
            def _():
                pass_on(0).start()
        else:
            direct(e).wait_recv()
            pass_on(e).start()

    for slot in range(1, steps, 2):
        arrival(slot).wait_recv()

    def sum_share(peer):
        rows = pl.ds(pl.multiple_of(peer * share, share), share)
        total = jnp.dot(adj[0, rows, :], gathered[0], preferred_element_type=jnp.float32)
        for o in range(1, steps):
            total = total + jnp.dot(
                adj[o, rows, :], gathered[o], preferred_element_type=jnp.float32
            )
        part[rows, :] = total

    def part_of(d):
        peer = lax.rem(rep + d, n_rep)
        return pltpu.make_async_remote_copy(
            src_ref=part.at[pl.ds(pl.multiple_of(peer * share, share), share)],
            dst_ref=precv.at[d - 1],
            send_sem=p_send.at[d - 1],
            recv_sem=p_recv.at[d - 1],
            device_id=(row, peer),
            device_id_type=MESH,
        )

    for d in range(1, n_rep):
        sum_share(lax.rem(rep + d, n_rep))
        part_of(d).start()
    sum_share(rep)

    for copy in loads[5:]:
        copy.wait()
    mine = pl.ds(pl.multiple_of(rep * share, share), share)
    sums = part[mine, :] + own[mine, :].astype(jnp.float32)
    for d in range(1, n_rep):
        part_of(d).wait()
        sums = sums + precv[d - 1]
    aggregate = (invb[mine, :] * sums).astype(jnp.bfloat16)
    x = jnp.dot(aggregate, w_ref[...], preferred_element_type=jnp.float32) + b_ref[...]
    x2 = x * x
    t = jnp.tanh(GELU_C * (x + GELU_A * (x2 * x)))
    cdf = 0.5 * (1.0 + t)
    act_ref[...] = (x * cdf).astype(jnp.bfloat16)
    slope = cdf + x * (0.5 * (1.0 - t * t)) * (GELU_C * (1.0 + (3.0 * GELU_A) * x2))
    delta = (cot_ref[...].astype(jnp.float32) * slope).astype(jnp.bfloat16)
    bias_sum = jnp.sum(delta.astype(jnp.float32), axis=0, keepdims=True)
    weight_sum = lax.dot_general(
        aggregate, delta, (((0,), (0,)), ((), ())), preferred_element_type=jnp.float32
    )
    for e in range(2, steps, 2):
        direct(e).wait_send()
        pass_on(e).wait_send()

    @pl.when(rep != 0)
    def _():
        direct(0).wait_send()

    @pl.when(core == 0)
    def _():
        across().wait_send()

    @pl.when(core == 1)
    def _():
        pass_on(0).wait_send()

    if not fuse_sum:
        gw_ref[...] = weight_sum
        gb_ref[...] = bias_sum
        return

    halves = weight_sum.shape[1] // BLK
    for p in range(n_dev):
        r0, c0 = p // halves * 8, p % halves * BLK
        gwp[p, 0:8, :] = weight_sum[r0 : r0 + 8, c0 : c0 + BLK]
        gwp[p, 8:9, :] = bias_sum[:, c0 : c0 + BLK]

    @pl.loop(1, n_dev)
    def _(d):
        p = lax.rem(me + d, n_dev)
        pltpu.make_async_remote_copy(
            src_ref=gwp.at[p],
            dst_ref=grecv.at[me],
            send_sem=g_send,
            recv_sem=g_recv,
            device_id=(p // n_rep, lax.rem(p, n_rep)),
            device_id_type=MESH,
        ).start()

    others = pl.ds(0, n_dev - 1)

    def all_of(src, dst, send_sem, recv_sem):
        p = lax.rem(me + 1, n_dev)
        return pltpu.make_async_remote_copy(
            src_ref=src.at[others],
            dst_ref=dst.at[others],
            send_sem=send_sem,
            recv_sem=recv_sem,
            device_id=(p // n_rep, lax.rem(p, n_rep)),
            device_id_type=MESH,
        )

    grecv[me] = gwp[me]
    all_of(gwp, grecv, g_send, g_recv).wait_recv()
    total = grecv[0]
    for s in range(1, n_dev):
        total = total + grecv[s]
    gfin[me] = total

    @pl.loop(1, n_dev)
    def _(d):
        p = lax.rem(me + d, n_dev)
        pltpu.make_async_remote_copy(
            src_ref=gfin.at[me],
            dst_ref=gfin.at[me],
            send_sem=o_send,
            recv_sem=o_recv,
            device_id=(p // n_rep, lax.rem(p, n_rep)),
            device_id_type=MESH,
        ).start()

    all_of(gwp, grecv, g_send, g_recv).wait_send()
    all_of(gfin, gfin, o_send, o_recv).wait_recv()
    for p in range(n_dev):
        r0, c0 = p // halves * 8, p % halves * BLK
        gw_ref[r0 : r0 + 8, c0 : c0 + BLK] = gfin[p, 0:8, :]
    for h in range(halves):
        gb_ref[:, h * BLK : (h + 1) * BLK] = gfin[h, 8:9, :]
    all_of(gfin, gfin, o_send, o_recv).wait_send()


def local(features, degree, tile_block, edge_count, edge_code, weight, bias, cotangent):
    n_rows = lax.axis_size("rows")
    n_rep = lax.axis_size("rep")
    n_dev = n_rows * n_rep
    blocks, steps, slots, ecap = edge_code.shape
    nodes, feat = features.shape
    hidden = weight.shape[1]
    share = nodes // n_rep
    fuse_sum = feat * hidden == n_dev * 8 * BLK
    held = n_dev if fuse_sum else 1
    hbm = pl.BlockSpec(memory_space=pltpu.HBM)
    vmem = pl.BlockSpec(memory_space=pltpu.VMEM)
    dma = pltpu.SemaphoreType.DMA
    others = max(n_rep - 1, 1)
    act, grad_w, grad_b = pl.pallas_call(
        functools.partial(kernel, n_rows, n_rep, fuse_sum),
        out_shape=(
            jax.ShapeDtypeStruct((share, hidden), jnp.bfloat16),
            jax.ShapeDtypeStruct((feat, hidden), jnp.float32),
            jax.ShapeDtypeStruct((1, hidden), jnp.float32),
        ),
        in_specs=[hbm] * 8,
        out_specs=(vmem, vmem, vmem),
        scratch_shapes=[
            pltpu.VMEM(features.shape, features.dtype),
            pltpu.VMEM((blocks, BLK), degree.dtype),
            pltpu.SMEM(tile_block.shape, tile_block.dtype),
            pltpu.SMEM(edge_count.shape, edge_count.dtype),
            pltpu.VMEM(edge_code.shape, edge_code.dtype),
            pltpu.VMEM(weight.shape, weight.dtype),
            pltpu.VMEM((1, hidden), bias.dtype),
            pltpu.VMEM(cotangent.shape, cotangent.dtype),
            pltpu.VMEM((nodes, feat), jnp.bfloat16),
            pltpu.VMEM((nodes, feat), jnp.float32),
            pltpu.VMEM((steps, nodes, nodes), jnp.bfloat16),
            pltpu.VMEM((steps, nodes, feat), jnp.bfloat16),
            pltpu.VMEM((nodes, feat), jnp.float32),
            pltpu.VMEM((others, share, feat), jnp.float32),
            pltpu.VMEM((held, 9, BLK), jnp.float32),
            pltpu.VMEM((held, 9, BLK), jnp.float32),
            pltpu.VMEM((held, 9, BLK), jnp.float32),
            dma((8,)),
            dma((steps // 2 + 1,)),
            dma((steps // 2,)),
            dma((steps,)),
            dma((others,)),
            dma((others,)),
            dma(()),
            dma(()),
            dma(()),
            dma(()),
        ],
        compiler_params=pltpu.CompilerParams(
            collective_id=0, has_side_effects=True, vmem_limit_bytes=65000 * 1024
        ),
    )(
        features,
        degree.reshape(blocks, BLK),
        tile_block,
        edge_count,
        edge_code,
        weight,
        bias.reshape(1, hidden),
        cotangent,
    )
    grad_b = grad_b.reshape(hidden)
    if not fuse_sum:
        grad_w, grad_b = lax.psum((grad_w, grad_b), ("rows", "rep"))
    return (act, grad_w, grad_b)


def solution(mesh):
    in_specs = (
        P("rows", None),
        P("rows"),
        P("rows", "rep", None),
        P("rows", "rep", None),
        P("rows", "rep", None, None),
        P(),
        P(),
        P(("rows", "rep"), None),
    )
    out_specs = (P(("rows", "rep"), None), P(), P())
    return jax.shard_map(local, mesh=mesh, in_specs=in_specs, out_specs=out_specs, check_vma=False)
```

time: 67.4 us -> 56.3 us (0.84)
  Pallas kernels: 58.8 us -> 52.6 us
  local copies, waits for them, and re-layouts: 7.54 us -> 2.85 us
    pallas_call x1, Pallas kernels: 58.8 us -> 52.6 us  [local(): pl.pallas_call(functools.partial(kernel, n_rows, n_rep, fuse_sum), out_sh...]
    unnamed x19 -> x7, local copies, waits for them, and re-layouts: 7.54 us -> 2.85 us
where the time goes in v2:
time: 56.3 us; the launch traced here: 56.1 us
  Pallas kernels  52.6 us (93%)
  local copies, waits for them, and re-layouts  2.85 us (5%)
  between operations  0.65 us (1%)
    pallas_call x1, Pallas kernels, local(): pl.pallas_call(functools.partial(kernel, n_rows, n_rep, fuse_sum), out_sh...  52.6 us
    unnamed x7, local copies, waits for them, and re-layouts  2.85 us

profile of v2, /device:TPU:0, one launch (start us, length us, event | category | flops | bytes accessed | tf_op | source)
XLA Modules:
  0.0 56.1 jit_solution(2740697511780288332)
XLA Ops:
  0.6 52.6 %shard_map.103 = (bf16[256,256]{1,0:T(8,128)(2,1)}, f32[128,256]{1,0:T(8,128)}, f32[1,256]{1,0:T(1,128)}) custom-call(bf16[512,128]{1,0:T(8,128)(2,1)} %feat_hbm.1, s32[4,128]{1,0:T(4,128)} %bitcast.3, s32[4,8,8]{2,1,0:T(8,128)} %tb_hbm.1, s32[4,8,8]{2,1,0:T(8,128)} %cnt_hbm.1, s32[4,8,8,128]{3,2,1,0:T(8,128)} %code_hbm.1, bf16[128,256]{1,0:T(8,128)(2,1)} %w_hbm.1, ...), custom_call_target="tpu_custom_call" | custom-call | tf_op jit(solution)/shard_map/pallas_call | solution.py:355
  53.2 0.0 copy-start
  53.3 1.6 %copy.14 = bf16[256,256]{1,0:T(8,128)(2,1)} copy(bf16[256,256]{1,0:T(8,128)(2,1)} %get-tuple-element.12) | data formatting | bytes 262144
  54.9 0.0 copy-done
  54.9 0.0 copy-start.1
  54.9 0.7 %copy.15 = f32[128,256]{1,0:T(8,128)} copy(f32[128,256]{1,0:T(8,128)S(1)} %copy-done) | data formatting | bytes 262144
  55.5 0.0 copy-done.1
  55.5 0.6 %copy.16 = f32[256]{0:T(256)} copy(f32[256]{0:T(256)S(1)} %bitcast.5) | data formatting | bytes 2048
Async XLA Ops:
  53.2 1.6 %copy-start = (f32[128,256]{1,0:T(8,128)S(1)}, f32[128,256]{1,0:T(8,128)}, u32[]{:S(2)}) copy-start(f32[128,256]{1,0:T(8,128)} %get-tuple-element.13) | copy-start | bytes 393220
  54.9 0.7 %copy-start.1 = (f32[1,256]{1,0:T(1,128)S(1)}, f32[1,256]{1,0:T(1,128)}, u32[]{:S(2)}) copy-start(f32[1,256]{1,0:T(1,128)} %get-tuple-element.8) | copy-start | bytes 3076

commit v3 on v2

--- a/solution.py
+++ b/solution.py
@@ -9,6 +9,7 @@
 
 MESH = pl.DeviceIdType.MESH
 BLK = 128
+LAYER = 8
 GELU_C = 0.7978845608028654
 GELU_A = 0.044715
 
@@ -18,8 +19,8 @@
     feat_hbm, deg_hbm, tb_hbm, cnt_hbm, code_hbm, w_hbm, b_hbm, cot_hbm,
     act_ref, gw_ref, gb_ref,
     feat_ref, deg_ref, tb_ref, cnt_ref, code_ref, w_ref, b_ref, cot_ref,
-    own, invb, adj, gathered, part, precv, gwp, grecv, gfin,
-    in_sem, d_send, f_send, s_recv, p_send, p_recv, g_send, g_recv, o_send, o_recv,
+    own, invb, adj, gathered, part, precv, gwp, grecv, zrecv, gfin,
+    in_sem, d_send, f_send, s_recv, p_send, p_recv, g_send, g_recv, z_send, z_recv, o_send, o_recv,
 ):
     blocks, steps, slots, ecap = code_ref.shape
     nodes = blocks * BLK
@@ -31,6 +32,20 @@
     me = row * n_rep + rep
     share = nodes // n_rep
     base = rep * steps
+
+    n_layers = n_dev // LAYER
+    place = lax.rem(me, LAYER)
+    layer = me // LAYER
+
+    def layer_peer(d):
+        at = lax.rem(place + d, LAYER)
+        p = layer * LAYER + at
+        return at, (p // n_rep, lax.rem(p, n_rep))
+
+    def layer_at(d):
+        at = lax.rem(layer + d, n_layers)
+        p = at * LAYER + place
+        return at, (p // n_rep, lax.rem(p, n_rep))
 
     def load(n, src, dst):
         return pltpu.make_async_copy(src, dst, in_sem.at[n])
@@ -58,25 +73,24 @@
     def greet(to_row, to_rep):
         pl.semaphore_signal(barrier, inc=1, device_id=(to_row, to_rep), device_id_type=MESH)
 
+    for e in range(2, steps, 2):
+        greet(lax.rem(row + base + e, n_rows), rep)
+
+    @pl.when(rep != 0)
+    def _():
+        greet(lax.rem(row + base, n_rows), rep)
+
+    @pl.when(core == 1)
+    def _():
+        greet(lax.rem(row + base + steps - 1, n_rows), rep)
+
     if fuse_sum:
-        @pl.loop(1, n_dev)
-        def _(d):
-            p = lax.rem(me + d, n_dev)
-            greet(p // n_rep, lax.rem(p, n_rep))
+        for d in range(1, LAYER):
+            greet(*layer_peer(d)[1])
+        for d in range(1, n_layers):
+            greet(*layer_at(d)[1])
     else:
-        for e in range(2, steps, 2):
-            greet(lax.rem(row + base + e, n_rows), rep)
-
-        @pl.when(rep != 0)
-        def _():
-            greet(lax.rem(row + base, n_rows), rep)
-
         greet(sibling, rep)
-
-        @pl.when(core == 1)
-        def _():
-            greet(lax.rem(row + base + steps - 1, n_rows), rep)
-
         for d in range(1, n_rep):
             greet(row, lax.rem(rep + d, n_rep))
 
@@ -90,18 +104,8 @@
         invb[rows, :] = wide
         own[rows, :] = (feat_ref[rows, :].astype(jnp.float32) * wide).astype(jnp.bfloat16)
 
-    if fuse_sum:
-        pl.semaphore_wait(barrier, n_dev - 1)
-    else:
-        pl.semaphore_wait(barrier, steps // 2 - 1 + 1 + n_rep - 1)
-
-        @pl.when(rep != 0)
-        def _():
-            pl.semaphore_wait(barrier, 1)
-
-        @pl.when(core == 0)
-        def _():
-            pl.semaphore_wait(barrier, 1)
+    fixed = LAYER - 1 + n_layers - 1 if fuse_sum else 1 + n_rep - 1
+    pl.semaphore_wait(barrier, steps // 2 - 1 + fixed + jnp.minimum(rep, 1) + 1 - core)
 
     def direct(e):
         return pltpu.make_async_remote_copy(
@@ -220,12 +224,12 @@
             total = total + jnp.dot(
                 adj[o, rows, :], gathered[o], preferred_element_type=jnp.float32
             )
-        part[rows, :] = total
+        return total
 
     def part_of(d):
         peer = lax.rem(rep + d, n_rep)
         return pltpu.make_async_remote_copy(
-            src_ref=part.at[pl.ds(pl.multiple_of(peer * share, share), share)],
+            src_ref=part.at[d - 1],
             dst_ref=precv.at[d - 1],
             send_sem=p_send.at[d - 1],
             recv_sem=p_recv.at[d - 1],
@@ -234,17 +238,17 @@
         )
 
     for d in range(1, n_rep):
-        sum_share(lax.rem(rep + d, n_rep))
+        part[d - 1] = sum_share(lax.rem(rep + d, n_rep)).astype(jnp.bfloat16)
         part_of(d).start()
-    sum_share(rep)
+    sums = sum_share(rep)
 
     for copy in loads[5:]:
         copy.wait()
     mine = pl.ds(pl.multiple_of(rep * share, share), share)
-    sums = part[mine, :] + own[mine, :].astype(jnp.float32)
+    sums = sums + own[mine, :].astype(jnp.float32)
     for d in range(1, n_rep):
         part_of(d).wait()
-        sums = sums + precv[d - 1]
+        sums = sums + precv[d - 1].astype(jnp.float32)
     aggregate = (invb[mine, :] * sums).astype(jnp.bfloat16)
     x = jnp.dot(aggregate, w_ref[...], preferred_element_type=jnp.float32) + b_ref[...]
     x2 = x * x
@@ -278,64 +282,95 @@
         gb_ref[...] = bias_sum
         return
 
-    halves = weight_sum.shape[1] // BLK
-    for p in range(n_dev):
-        r0, c0 = p // halves * 8, p % halves * BLK
-        gwp[p, 0:8, :] = weight_sum[r0 : r0 + 8, c0 : c0 + BLK]
-        gwp[p, 8:9, :] = bias_sum[:, c0 : c0 + BLK]
-
-    @pl.loop(1, n_dev)
-    def _(d):
-        p = lax.rem(me + d, n_dev)
-        pltpu.make_async_remote_copy(
-            src_ref=gwp.at[p],
-            dst_ref=grecv.at[me],
-            send_sem=g_send,
-            recv_sem=g_recv,
-            device_id=(p // n_rep, lax.rem(p, n_rep)),
-            device_id_type=MESH,
-        ).start()
-
-    others = pl.ds(0, n_dev - 1)
-
-    def all_of(src, dst, send_sem, recv_sem):
-        p = lax.rem(me + 1, n_dev)
-        return pltpu.make_async_remote_copy(
-            src_ref=src.at[others],
-            dst_ref=dst.at[others],
-            send_sem=send_sem,
-            recv_sem=recv_sem,
-            device_id=(p // n_rep, lax.rem(p, n_rep)),
-            device_id_type=MESH,
-        )
-
-    grecv[me] = gwp[me]
-    all_of(gwp, grecv, g_send, g_recv).wait_recv()
+    depth = weight_sum.shape[0] // LAYER
+    for p in range(LAYER):
+        gwp[p, 0:depth, :] = weight_sum[p * depth : (p + 1) * depth, :]
+        gwp[p, depth : depth + 1, :] = bias_sum
+
+    def scatter(d):
+        at, device = layer_peer(d)
+        return pltpu.make_async_remote_copy(
+            src_ref=gwp.at[at],
+            dst_ref=grecv.at[place],
+            send_sem=g_send.at[d - 1],
+            recv_sem=g_recv.at[d - 1],
+            device_id=device,
+            device_id_type=MESH,
+        )
+
+    def swap(d):
+        return pltpu.make_async_remote_copy(
+            src_ref=zrecv.at[layer],
+            dst_ref=zrecv.at[layer],
+            send_sem=z_send.at[d - 1],
+            recv_sem=z_recv.at[d - 1],
+            device_id=layer_at(d)[1],
+            device_id_type=MESH,
+        )
+
+    def spread(d):
+        return pltpu.make_async_remote_copy(
+            src_ref=gfin.at[place],
+            dst_ref=gfin.at[place],
+            send_sem=o_send.at[d - 1],
+            recv_sem=o_recv.at[d - 1],
+            device_id=layer_peer(d)[1],
+            device_id_type=MESH,
+        )
+
+    for d in range(1, LAYER):
+        scatter(d).start()
+    grecv[place] = gwp[place]
+    for d in range(1, LAYER):
+        scatter(d).wait_recv()
     total = grecv[0]
-    for s in range(1, n_dev):
+    for s in range(1, LAYER):
         total = total + grecv[s]
-    gfin[me] = total
-
-    @pl.loop(1, n_dev)
-    def _(d):
-        p = lax.rem(me + d, n_dev)
-        pltpu.make_async_remote_copy(
-            src_ref=gfin.at[me],
-            dst_ref=gfin.at[me],
-            send_sem=o_send,
-            recv_sem=o_recv,
-            device_id=(p // n_rep, lax.rem(p, n_rep)),
-            device_id_type=MESH,
-        ).start()
-
-    all_of(gwp, grecv, g_send, g_recv).wait_send()
-    all_of(gfin, gfin, o_send, o_recv).wait_recv()
-    for p in range(n_dev):
-        r0, c0 = p // halves * 8, p % halves * BLK
-        gw_ref[r0 : r0 + 8, c0 : c0 + BLK] = gfin[p, 0:8, :]
-    for h in range(halves):
-        gb_ref[:, h * BLK : (h + 1) * BLK] = gfin[h, 8:9, :]
-    all_of(gfin, gfin, o_send, o_recv).wait_send()
+    zrecv[layer] = total
+    for d in range(1, n_layers):
+        swap(d).start()
+    for d in range(1, n_layers):
+        swap(d).wait_recv()
+    total = zrecv[0]
+    for s in range(1, n_layers):
+        total = total + zrecv[s]
+    gfin[place] = total
+    for d in range(1, LAYER):
+        spread(d).start()
+    gb_ref[...] = total[depth : depth + 1, :]
+    for d in range(1, LAYER):
+        scatter(d).wait_send()
+    for d in range(1, n_layers):
+        swap(d).wait_send()
+    for d in range(1, LAYER):
+        spread(d).wait_recv()
+    for p in range(LAYER):
+        gw_ref[p * depth : (p + 1) * depth, :] = gfin[p, 0:depth, :]
+    for d in range(1, LAYER):
+        spread(d).wait_send()
+
+
+def finish_kernel(a_ref, b_ref, c_ref, a_out, b_out, c_out, sem):
+    copies = [
+        pltpu.make_async_copy(src, dst, sem.at[n])
+        for n, (src, dst) in enumerate(((a_ref, a_out), (b_ref, b_out), (c_ref, c_out)))
+    ]
+    for copy in copies:
+        copy.start()
+    for copy in copies:
+        copy.wait()
+
+
+def finish(*results):
+    hbm = pl.BlockSpec(memory_space=pltpu.HBM)
+    return pl.pallas_call(
+        finish_kernel,
+        out_shape=tuple(jax.ShapeDtypeStruct(r.shape, r.dtype) for r in results),
+        in_specs=[hbm] * 3,
+        out_specs=(hbm,) * 3,
+        scratch_shapes=[pltpu.SemaphoreType.DMA((3,))],
+        compiler_params=pltpu.CompilerParams(vmem_limit_bytes=65000 * 1024),
+    )(*results)
 
 
 def local(features, degree, tile_block, edge_count, edge_code, weight, bias, cotangent):
@@ -346,8 +381,9 @@
     nodes, feat = features.shape
     hidden = weight.shape[1]
     share = nodes // n_rep
-    fuse_sum = feat * hidden == n_dev * 8 * BLK
-    held = n_dev if fuse_sum else 1
+    fuse_sum = n_dev % LAYER == 0 and n_dev <= 8 * LAYER and LAYER % n_rep == 0 and feat % (8 * LAYER) == 0
+    n_layers = n_dev // LAYER if fuse_sum else 1
+    depth = feat // LAYER + 1
     hbm = pl.BlockSpec(memory_space=pltpu.HBM)
     vmem = pl.BlockSpec(memory_space=pltpu.VMEM)
     dma = pltpu.SemaphoreType.DMA
@@ -374,21 +410,24 @@
             pltpu.VMEM((nodes, feat), jnp.float32),
             pltpu.VMEM((steps, nodes, nodes), jnp.bfloat16),
             pltpu.VMEM((steps, nodes, feat), jnp.bfloat16),
-            pltpu.VMEM((nodes, feat), jnp.float32),
-            pltpu.VMEM((others, share, feat), jnp.float32),
-            pltpu.VMEM((held, 9, BLK), jnp.float32),
-            pltpu.VMEM((held, 9, BLK), jnp.float32),
-            pltpu.VMEM((held, 9, BLK), jnp.float32),
+            pltpu.VMEM((others, share, feat), jnp.bfloat16),
+            pltpu.VMEM((others, share, feat), jnp.bfloat16),
+            pltpu.VMEM((LAYER, depth, hidden), jnp.float32),
+            pltpu.VMEM((LAYER, depth, hidden), jnp.float32),
+            pltpu.VMEM((n_layers, depth, hidden), jnp.float32),
+            pltpu.VMEM((LAYER, depth, hidden), jnp.float32),
             dma((8,)),
             dma((steps // 2 + 1,)),
             dma((steps // 2,)),
             dma((steps,)),
             dma((others,)),
             dma((others,)),
-            dma(()),
-            dma(()),
-            dma(()),
-            dma(()),
+            dma((LAYER - 1,)),
+            dma((LAYER - 1,)),
+            dma((max(n_layers - 1, 1),)),
+            dma((max(n_layers - 1, 1),)),
+            dma((LAYER - 1,)),
+            dma((LAYER - 1,)),
         ],
         compiler_params=pltpu.CompilerParams(
             collective_id=0, has_side_effects=True, vmem_limit_bytes=65000 * 1024
@@ -403,6 +442,8 @@
         bias.reshape(1, hidden),
         cotangent,
     )
+    if fuse_sum:
+        act, grad_w, grad_b = finish(act, grad_w, grad_b)
     grad_b = grad_b.reshape(hidden)
     if not fuse_sum:
         grad_w, grad_b = lax.psum((grad_w, grad_b), ("rows", "rep"))

time: 56.3 us -> 59 us (1.048); the launches traced: 56.1 us -> 58 us
  Pallas kernels: 52.6 us -> 57.4 us
  local copies, waits for them, and re-layouts: 2.85 us -> 0 us
    pallas_call x0 -> x1, Pallas kernels: none -> 9.1 us  [finish(): pl.pallas_call(finish_kernel, out_shape=tuple((jax.ShapeDtypeStruct(r.sha...]
    pallas_call x1, Pallas kernels: 52.6 us -> 48.3 us  [local(): pl.pallas_call(functools.partial(kernel, n_rows, n_rep, fuse_sum), out_sh...]
    unnamed x7 -> x0, local copies, waits for them, and re-layouts: 2.85 us -> none
where the time goes in v3:
time: 59 us; the launch traced here: 58 us
  Pallas kernels  57.4 us (97%)
  between operations  0.64 us (1%)
    pallas_call x1, Pallas kernels, local(): pl.pallas_call(functools.partial(kernel, n_rows, n_rep, fuse_sum), out_sh...  48.3 us
    pallas_call x1, Pallas kernels, finish(): pl.pallas_call(finish_kernel, out_shape=tuple((jax.ShapeDtypeStruct(r.sha...  9.1 us

profile of v3, /device:TPU:0, one launch (start us, length us, event | category | flops | bytes accessed | tf_op | source)
XLA Modules:
  0.0 58.0 jit_solution(8327478530205649397)
XLA Ops:
  0.6 48.3 %shard_map.103 = (bf16[256,256]{1,0:T(8,128)(2,1)}, f32[128,256]{1,0:T(8,128)}, f32[1,256]{1,0:T(1,128)}) custom-call(bf16[512,128]{1,0:T(8,128)(2,1)} %feat_hbm.1, s32[4,128]{1,0:T(4,128)} %bitcast.3, s32[4,8,8]{2,1,0:T(8,128)} %tb_hbm.1, s32[4,8,8]{2,1,0:T(8,128)} %cnt_hbm.1, s32[4,8,8,128]{3,2,1,0:T(8,128)} %code_hbm.1, bf16[128,256]{1,0:T(8,128)(2,1)} %w_hbm.1, ...), custom_call_target="tpu_custom_call" | custom-call | tf_op jit(solution)/shard_map/pallas_call | solution.py:391
  48.9 9.1 %shard_map.104 = (bf16[256,256]{1,0:T(8,128)(2,1)}, f32[128,256]{1,0:T(8,128)}, f32[1,256]{1,0:T(1,128)}) custom-call(bf16[256,256]{1,0:T(8,128)(2,1)} %get-tuple-element.9.a_ref, f32[128,256]{1,0:T(8,128)} %get-tuple-element.10.b_ref, f32[1,256]{1,0:T(1,128)} %get-tuple-element.11.c_ref), custom_call_target="tpu_custom_call" | custom-call | tf_op jit(solution)/shard_map/pallas_call | solution.py:366

commit v4 on v3

--- a/solution.py
+++ b/solution.py
@@ -170,28 +170,28 @@
     for copy in loads[2:5]:
         copy.wait()
 
-    def hot(index):
-        index = jnp.broadcast_to(index.astype(jnp.float32), (BLK, ecap)).astype(jnp.bfloat16)
-        return jnp.where(sub == index, one, zero)
+    lane_of = lax.broadcasted_iota(jnp.int32, (ecap, BLK), 1).astype(jnp.float32).astype(jnp.bfloat16)
 
     def build(t):
         i = t // steps
         o = lax.rem(t, steps)
         codes = code_ref[i, o]
-        targets, fars = [], []
+        fars = (codes & (BLK - 1)).astype(jnp.float32).T
+        targets, hits = [], []
         for k in range(slots):
-            code = codes[k : k + 1, :]
-            far = code & (BLK - 1)
-            targets.append(hot(jnp.where(lane < cnt_ref[i, o, k], code >> 7, -1)))
-            fars.append(
-                jnp.concatenate(
-                    [hot(jnp.where(tb_ref[i, o, k] == q, far, -1)) for q in range(blocks)], axis=0
-                )
-            )
-        tile = lax.dot_general(
+            target = jnp.where(lane < cnt_ref[i, o, k], codes[k : k + 1, :] >> 7, -1)
+            target = jnp.broadcast_to(target.astype(jnp.float32), (BLK, ecap)).astype(jnp.bfloat16)
+            targets.append(jnp.where(sub == target, one, zero))
+            far = jnp.broadcast_to(fars[:, k : k + 1], (ecap, BLK)).astype(jnp.bfloat16)
+            hit = far == lane_of
+            marks = [
+                jnp.full((ecap, BLK), jnp.where(tb_ref[i, o, k] == q, 1.0, 0.0)).astype(jnp.bfloat16)
+                for q in range(blocks)
+            ]
+            hits.append(jnp.concatenate([jnp.where(hit, mark, zero) for mark in marks], axis=1))
+        tile = jnp.dot(
             jnp.concatenate(targets, axis=1),
-            jnp.concatenate(fars, axis=1),
-            (((1,), (1,)), ((), ())),
+            jnp.concatenate(hits, axis=0),
             preferred_element_type=jnp.float32,
         )
         adj[o, pl.ds(pl.multiple_of(i * BLK, BLK), BLK), :] = tile.astype(jnp.bfloat16)
@@ -350,14 +350,16 @@
         spread(d).wait_send()
 
 
-def finish_kernel(a_ref, b_ref, c_ref, a_out, b_out, c_out, sem):
-    copies = [
-        pltpu.make_async_copy(src, dst, sem.at[n])
-        for n, (src, dst) in enumerate(((a_ref, a_out), (b_ref, b_out), (c_ref, c_out)))
-    ]
-    for copy in copies:
+def finish_kernel(a_ref, b_ref, c_ref, a_out, b_out, c_out, a_mid, b_mid, c_mid, sem_in, sem_out):
+    plan = ((a_ref, a_mid, a_out), (b_ref, b_mid, b_out), (c_ref, c_mid, c_out))
+    loads = [pltpu.make_async_copy(src, mid, sem_in.at[n]) for n, (src, mid, _) in enumerate(plan)]
+    stores = [pltpu.make_async_copy(mid, dst, sem_out.at[n]) for n, (_, mid, dst) in enumerate(plan)]
+    for copy in loads:
         copy.start()
-    for copy in copies:
+    for load, store in zip(loads, stores):
+        load.wait()
+        store.start()
+    for copy in stores:
         copy.wait()
 
 
@@ -368,7 +370,8 @@
         out_shape=tuple(jax.ShapeDtypeStruct(r.shape, r.dtype) for r in results),
         in_specs=[hbm] * 3,
         out_specs=(hbm,) * 3,
-        scratch_shapes=[pltpu.SemaphoreType.DMA((3,))],
+        scratch_shapes=[pltpu.VMEM(r.shape, r.dtype) for r in results]
+        + [pltpu.SemaphoreType.DMA((3,)), pltpu.SemaphoreType.DMA((3,))],
         compiler_params=pltpu.CompilerParams(vmem_limit_bytes=65000 * 1024),
     )(*results)
 

time: 59 us -> 51.3 us (0.87)
  Pallas kernels: 57.4 us -> 49.6 us
    pallas_call x1, Pallas kernels: 9.1 us -> 1.68 us  [finish(): pl.pallas_call(finish_kernel, out_shape=tuple((jax.ShapeDtypeStruct(r.sha...]
where the time goes in v4:
time: 51.3 us; the launch traced here: 50.3 us
  Pallas kernels  49.6 us (97%)
  between operations  0.64 us (1%)
    pallas_call x1, Pallas kernels, local(): pl.pallas_call(functools.partial(kernel, n_rows, n_rep, fuse_sum), out_sh...  47.9 us
    pallas_call x1, Pallas kernels, finish(): pl.pallas_call(finish_kernel, out_shape=tuple((jax.ShapeDtypeStruct(r.sha...  1.68 us

profile of v4, /device:TPU:0, one launch (start us, length us, event | category | flops | bytes accessed | tf_op | source)
XLA Modules:
  0.0 50.3 jit_solution(6176594701987447938)
XLA Ops:
  0.6 47.9 %shard_map.103 = (bf16[256,256]{1,0:T(8,128)(2,1)}, f32[128,256]{1,0:T(8,128)}, f32[1,256]{1,0:T(1,128)}) custom-call(bf16[512,128]{1,0:T(8,128)(2,1)} %feat_hbm.1, s32[4,128]{1,0:T(4,128)} %bitcast.3, s32[4,8,8]{2,1,0:T(8,128)} %tb_hbm.1, s32[4,8,8]{2,1,0:T(8,128)} %cnt_hbm.1, s32[4,8,8,128]{3,2,1,0:T(8,128)} %code_hbm.1, bf16[128,256]{1,0:T(8,128)(2,1)} %w_hbm.1, ...), custom_call_target="tpu_custom_call" | custom-call | tf_op jit(solution)/shard_map/pallas_call | solution.py:394
  48.6 1.7 %shard_map.104 = (bf16[256,256]{1,0:T(8,128)(2,1)}, f32[128,256]{1,0:T(8,128)}, f32[1,256]{1,0:T(1,128)}) custom-call(bf16[256,256]{1,0:T(8,128)(2,1)} %get-tuple-element.9.a_ref, f32[128,256]{1,0:T(8,128)} %get-tuple-element.10.b_ref, f32[1,256]{1,0:T(1,128)} %get-tuple-element.11.c_ref), custom_call_target="tpu_custom_call" | custom-call | tf_op jit(solution)/shard_map/pallas_call | solution.py:368

commit v5 on v4

--- a/solution.py
+++ b/solution.py
@@ -10,6 +10,7 @@
 MESH = pl.DeviceIdType.MESH
 BLK = 128
 LAYER = 8
+SEATS = 4
 GELU_C = 0.7978845608028654
 GELU_A = 0.044715
 
@@ -27,11 +28,10 @@
     n_dev = n_rows * n_rep
     row = lax.axis_index("rows")
     rep = lax.axis_index("rep")
-    core = lax.rem(row, 2)
-    sibling = row + 1 - 2 * core
+    seat = lax.rem(row, SEATS)
+    last = n_rep - 1
     me = row * n_rep + rep
     share = nodes // n_rep
-    base = rep * steps
 
     n_layers = n_dev // LAYER
     place = lax.rem(me, LAYER)
@@ -46,6 +46,20 @@
         at = lax.rem(layer + d, n_layers)
         p = at * LAYER + place
         return at, (p // n_rep, lax.rem(p, n_rep))
+
+    def comes(t):
+        if t == 0:
+            return rep != 0
+        if t == 1:
+            return rep >= 0
+        return jnp.logical_and(rep != last, seat != SEATS - 1)
+
+    def shared(t, to):
+        if t == 0:
+            return to < seat
+        if t == 1:
+            return to != seat
+        return to > seat
 
     def load(n, src, dst):
         return pltpu.make_async_copy(src, dst, in_sem.at[n])
@@ -73,24 +87,18 @@
     def greet(to_row, to_rep):
         pl.semaphore_signal(barrier, inc=1, device_id=(to_row, to_rep), device_id_type=MESH)
 
-    for e in range(2, steps, 2):
-        greet(lax.rem(row + base + e, n_rows), rep)
-
-    @pl.when(rep != 0)
-    def _():
-        greet(lax.rem(row + base, n_rows), rep)
-
-    @pl.when(core == 1)
-    def _():
-        greet(lax.rem(row + base + steps - 1, n_rows), rep)
-
     if fuse_sum:
         for d in range(1, LAYER):
             greet(*layer_peer(d)[1])
         for d in range(1, n_layers):
             greet(*layer_at(d)[1])
     else:
-        greet(sibling, rep)
+        for t in range(3):
+            @pl.when(comes(t))
+            def _(t=t):
+                greet(lax.rem(row + SEATS * (2 * rep + t), n_rows), rep)
+        for d in range(1, SEATS):
+            greet(row - seat + lax.rem(seat + d, SEATS), rep)
         for d in range(1, n_rep):
             greet(row, lax.rem(rep + d, n_rep))
 
@@ -104,39 +112,44 @@
         invb[rows, :] = wide
         own[rows, :] = (feat_ref[rows, :].astype(jnp.float32) * wide).astype(jnp.bfloat16)
 
-    fixed = LAYER - 1 + n_layers - 1 if fuse_sum else 1 + n_rep - 1
-    pl.semaphore_wait(barrier, steps // 2 - 1 + fixed + jnp.minimum(rep, 1) + 1 - core)
-
-    def direct(e):
+    if fuse_sum:
+        pl.semaphore_wait(barrier, LAYER - 1 + n_layers - 1)
+    else:
+        third = jnp.minimum(last - rep, 1) * jnp.minimum(SEATS - 1 - seat, 1)
+        pl.semaphore_wait(barrier, SEATS - 1 + n_rep - 1 + 1 + jnp.minimum(rep, 1) + third)
+
+    def direct(t):
         return pltpu.make_async_remote_copy(
             src_ref=own,
-            dst_ref=gathered.at[e],
-            send_sem=d_send.at[e // 2],
-            recv_sem=s_recv.at[e],
-            device_id=(lax.rem(row + n_rows - base - e, n_rows), rep),
-            device_id_type=MESH,
-        )
-
-    def across():
-        return pltpu.make_async_remote_copy(
-            src_ref=own,
-            dst_ref=gathered.at[steps - 1],
-            send_sem=d_send.at[steps // 2],
-            recv_sem=s_recv.at[steps - 1],
-            device_id=(lax.rem(row + n_rows - base - steps + 1, n_rows), rep),
-            device_id_type=MESH,
-        )
-
-    def pass_on(e):
-        slot = e - 1 + 2 * core
-        return pltpu.make_async_remote_copy(
-            src_ref=gathered.at[e],
+            dst_ref=gathered.at[SEATS * t],
+            send_sem=d_send.at[t],
+            recv_sem=s_recv.at[SEATS * t],
+            device_id=(lax.rem(row + 2 * n_rows - SEATS * (2 * rep + t), n_rows), rep),
+            device_id_type=MESH,
+        )
+
+    def pass_on(t, to):
+        slot = SEATS * t + seat - to
+        return pltpu.make_async_remote_copy(
+            src_ref=gathered.at[SEATS * t],
             dst_ref=gathered.at[slot],
-            send_sem=f_send.at[e // 2],
+            send_sem=f_send.at[SEATS * t + to],
             recv_sem=s_recv.at[slot],
-            device_id=(sibling, rep),
-            device_id_type=MESH,
-        )
+            device_id=(row - seat + to, rep),
+            device_id_type=MESH,
+        )
+
+    def share_out(t):
+        for to in range(SEATS):
+            @pl.when(shared(t, to))
+            def _(to=to):
+                pass_on(t, to).start()
+
+    def land(t):
+        @pl.when(comes(t))
+        def _():
+            direct(t).wait_recv()
+            share_out(t)
 
     def arrival(slot):
         return pltpu.make_async_remote_copy(
@@ -144,24 +157,24 @@
             dst_ref=gathered.at[slot],
             send_sem=d_send.at[0],
             recv_sem=s_recv.at[slot],
-            device_id=(sibling, rep),
-            device_id_type=MESH,
-        )
-
-    @pl.when(rep != 0)
-    def _():
-        direct(0).start()
-
-    for e in range(2, steps, 2):
-        direct(e).start()
-
-    @pl.when(core == 0)
-    def _():
-        across().start()
+            device_id=(row - seat + lax.rem(seat + 1, SEATS), rep),
+            device_id_type=MESH,
+        )
+
+    for t in (1, 0, 2):
+        @pl.when(comes(t))
+        def _(t=t):
+            direct(t).start()
 
     @pl.when(rep == 0)
     def _():
         gathered[0] = own[...]
+        share_out(0)
+
+    @pl.when(rep == last)
+    def _():
+        gathered[2 * SEATS] = own[...]
+        share_out(2)
 
     sub = lax.broadcasted_iota(jnp.int32, (BLK, ecap), 0).astype(jnp.float32).astype(jnp.bfloat16)
     lane = lax.broadcasted_iota(jnp.int32, (1, ecap), 1)
@@ -196,26 +209,19 @@
         )
         adj[o, pl.ds(pl.multiple_of(i * BLK, BLK), BLK), :] = tile.astype(jnp.bfloat16)
 
-    chunk = blocks * steps // (steps // 2)
-    for e in range(0, steps, 2):
-        @pl.loop(e // 2 * chunk, (e // 2 + 1) * chunk)
+    total_steps = blocks * steps
+    cuts = (0, total_steps * 3 // 8, total_steps * 11 // 16, total_steps)
+    for part_index, ready in enumerate(((1,), (0, 2), ())):
+        @pl.loop(cuts[part_index], cuts[part_index + 1])
         def _(t):
             build(t)
 
-        if e == 0:
-            @pl.when(rep != 0)
-            def _():
-                direct(0).wait_recv()
-
-            @pl.when(core == 1)
-            def _():
-                pass_on(0).start()
-        else:
-            direct(e).wait_recv()
-            pass_on(e).start()
-
-    for slot in range(1, steps, 2):
-        arrival(slot).wait_recv()
+        for t in ready:
+            land(t)
+
+    for slot in range(1, steps):
+        if slot % SEATS:
+            arrival(slot).wait_recv()
 
     def sum_share(peer):
         rows = pl.ds(pl.multiple_of(peer * share, share), share)
@@ -261,21 +267,19 @@
     weight_sum = lax.dot_general(
         aggregate, delta, (((0,), (0,)), ((), ())), preferred_element_type=jnp.float32
     )
-    for e in range(2, steps, 2):
-        direct(e).wait_send()
-        pass_on(e).wait_send()
-
-    @pl.when(rep != 0)
-    def _():
-        direct(0).wait_send()
-
-    @pl.when(core == 0)
-    def _():
-        across().wait_send()
-
-    @pl.when(core == 1)
-    def _():
-        pass_on(0).wait_send()
+    for t in range(3):
+        @pl.when(comes(t))
+        def _(t=t):
+            direct(t).wait_send()
+
+        for to in range(SEATS):
+            held = shared(t, to)
+            if t == 2:
+                held = jnp.logical_and(held, jnp.logical_or(comes(t), rep == last))
+
+            @pl.when(held)
+            def _(t=t, to=to):
+                pass_on(t, to).wait_send()
 
     if not fuse_sum:
         gw_ref[...] = weight_sum
@@ -412,7 +416,7 @@
             pltpu.VMEM((nodes, feat), jnp.bfloat16),
             pltpu.VMEM((nodes, feat), jnp.float32),
             pltpu.VMEM((steps, nodes, nodes), jnp.bfloat16),
-            pltpu.VMEM((steps, nodes, feat), jnp.bfloat16),
+            pltpu.VMEM((steps + 1, nodes, feat), jnp.bfloat16),
             pltpu.VMEM((others, share, feat), jnp.bfloat16),
             pltpu.VMEM((others, share, feat), jnp.bfloat16),
             pltpu.VMEM((LAYER, depth, hidden), jnp.float32),
@@ -420,9 +424,9 @@
             pltpu.VMEM((n_layers, depth, hidden), jnp.float32),
             pltpu.VMEM((LAYER, depth, hidden), jnp.float32),
             dma((8,)),
-            dma((steps // 2 + 1,)),
-            dma((steps // 2,)),
-            dma((steps,)),
+            dma((3,)),
+            dma((3 * SEATS,)),
+            dma((steps + 1,)),
             dma((others,)),
             dma((others,)),
             dma((LAYER - 1,)),

time: 51.3 us -> 43.4 us (0.85); the launches traced: 50.3 us -> 43.3 us
  Pallas kernels: 49.6 us -> 42.6 us
    pallas_call x1, Pallas kernels: 47.9 us -> 41 us  [local(): pl.pallas_call(functools.partial(kernel, n_rows, n_rep, fuse_sum), out_sh...]
where the time goes in v5:
time: 43.4 us; the launch traced here: 43.3 us
  Pallas kernels  42.6 us (98%)
  between operations  0.64 us (1%)
    pallas_call x1, Pallas kernels, local(): pl.pallas_call(functools.partial(kernel, n_rows, n_rep, fuse_sum), out_sh...  41 us
    pallas_call x1, Pallas kernels, finish(): pl.pallas_call(finish_kernel, out_shape=tuple((jax.ShapeDtypeStruct(r.sha...  1.68 us

profile of v5, /device:TPU:0, one launch (start us, length us, event | category | flops | bytes accessed | tf_op | source)
XLA Modules:
  0.0 43.3 jit_solution(13015112632905042492)
XLA Ops:
  0.6 41.0 %shard_map.103 = (bf16[256,256]{1,0:T(8,128)(2,1)}, f32[128,256]{1,0:T(8,128)}, f32[1,256]{1,0:T(1,128)}) custom-call(bf16[512,128]{1,0:T(8,128)(2,1)} %feat_hbm.1, s32[4,128]{1,0:T(4,128)} %bitcast.3, s32[4,8,8]{2,1,0:T(8,128)} %tb_hbm.1, s32[4,8,8]{2,1,0:T(8,128)} %cnt_hbm.1, s32[4,8,8,128]{3,2,1,0:T(8,128)} %code_hbm.1, bf16[128,256]{1,0:T(8,128)(2,1)} %w_hbm.1, ...), custom_call_target="tpu_custom_call" | custom-call | tf_op jit(solution)/shard_map/pallas_call | solution.py:398
  41.6 1.7 %shard_map.104 = (bf16[256,256]{1,0:T(8,128)(2,1)}, f32[128,256]{1,0:T(8,128)}, f32[1,256]{1,0:T(1,128)}) custom-call(bf16[256,256]{1,0:T(8,128)(2,1)} %get-tuple-element.9.a_ref, f32[128,256]{1,0:T(8,128)} %get-tuple-element.10.b_ref, f32[1,256]{1,0:T(1,128)} %get-tuple-element.11.c_ref), custom_call_target="tpu_custom_call" | custom-call | tf_op jit(solution)/shard_map/pallas_call | solution.py:372

commit v6 on v5

--- a/solution.py
+++ b/solution.py
@@ -18,9 +18,9 @@
 def kernel(
     n_rows, n_rep, fuse_sum,
     feat_hbm, deg_hbm, tb_hbm, cnt_hbm, code_hbm, w_hbm, b_hbm, cot_hbm,
-    act_ref, gw_ref, gb_ref,
+    act_hbm, gw_hbm, gb_hbm,
     feat_ref, deg_ref, tb_ref, cnt_ref, code_ref, w_ref, b_ref, cot_ref,
-    own, invb, adj, gathered, part, precv, gwp, grecv, zrecv, gfin,
+    act, gb, acc, out_sem, own, invb, adj, gathered, part, precv, gwp, grecv, zrecv, gfin,
     in_sem, d_send, f_send, s_recv, p_send, p_recv, g_send, g_recv, z_send, z_recv, o_send, o_recv,
 ):
     blocks, steps, slots, ecap = code_ref.shape
@@ -219,18 +219,27 @@
         for t in ready:
             land(t)
 
-    for slot in range(1, steps):
-        if slot % SEATS:
-            arrival(slot).wait_recv()
+    def turn(s):
+        o = jnp.where(rep == last, steps - 1 - s, s)
+
+        @pl.when(lax.rem(o, SEATS) != 0)
+        def _():
+            arrival(o).wait_recv()
+
+        return o
+
+    for s in range(steps - 1):
+        o = turn(s)
+        term = jnp.dot(adj[o], gathered[o], preferred_element_type=jnp.float32)
+        acc[...] = acc[...] + term if s else term
+
+    final = turn(steps - 1)
 
     def sum_share(peer):
         rows = pl.ds(pl.multiple_of(peer * share, share), share)
-        total = jnp.dot(adj[0, rows, :], gathered[0], preferred_element_type=jnp.float32)
-        for o in range(1, steps):
-            total = total + jnp.dot(
-                adj[o, rows, :], gathered[o], preferred_element_type=jnp.float32
-            )
-        return total
+        return acc[rows, :] + jnp.dot(
+            adj[final, rows, :], gathered[final], preferred_element_type=jnp.float32
+        )
 
     def part_of(d):
         peer = lax.rem(rep + d, n_rep)
@@ -260,7 +269,9 @@
     x2 = x * x
     t = jnp.tanh(GELU_C * (x + GELU_A * (x2 * x)))
     cdf = 0.5 * (1.0 + t)
-    act_ref[...] = (x * cdf).astype(jnp.bfloat16)
+    act[...] = (x * cdf).astype(jnp.bfloat16)
+    act_out = pltpu.make_async_copy(act, act_hbm, out_sem.at[0])
+    act_out.start()
     slope = cdf + x * (0.5 * (1.0 - t * t)) * (GELU_C * (1.0 + (3.0 * GELU_A) * x2))
     delta = (cot_ref[...].astype(jnp.float32) * slope).astype(jnp.bfloat16)
     bias_sum = jnp.sum(delta.astype(jnp.float32), axis=0, keepdims=True)
@@ -282,8 +293,17 @@
                 pass_on(t, to).wait_send()
 
     if not fuse_sum:
-        gw_ref[...] = weight_sum
-        gb_ref[...] = bias_sum
+        gw = gwp.at[0, pl.ds(0, weight_sum.shape[0])]
+        gw[...] = weight_sum
+        gb[...] = bias_sum
+        outs = [
+            pltpu.make_async_copy(gw, gw_hbm, out_sem.at[2]),
+            pltpu.make_async_copy(gb, gb_hbm, out_sem.at[1]),
+        ]
+        for copy in outs:
+            copy.start()
+        for copy in outs + [act_out]:
+            copy.wait()
         return
 
     depth = weight_sum.shape[0] // LAYER
@@ -341,17 +361,27 @@
     gfin[place] = total
     for d in range(1, LAYER):
         spread(d).start()
-    gb_ref[...] = total[depth : depth + 1, :]
+    gb[...] = total[depth : depth + 1, :]
+    gb_out = pltpu.make_async_copy(gb, gb_hbm, out_sem.at[1])
+    gb_out.start()
+    gw_outs = [
+        pltpu.make_async_copy(
+            gfin.at[p, pl.ds(0, depth)], gw_hbm.at[pl.ds(p * depth, depth)], out_sem.at[2 + p]
+        )
+        for p in range(LAYER)
+    ]
     for d in range(1, LAYER):
         scatter(d).wait_send()
     for d in range(1, n_layers):
         swap(d).wait_send()
     for d in range(1, LAYER):
         spread(d).wait_recv()
-    for p in range(LAYER):
-        gw_ref[p * depth : (p + 1) * depth, :] = gfin[p, 0:depth, :]
+    for copy in gw_outs:
+        copy.start()
     for d in range(1, LAYER):
         spread(d).wait_send()
+    for copy in gw_outs + [gb_out, act_out]:
+        copy.wait()
 
 
 def finish_kernel(a_ref, b_ref, c_ref, a_out, b_out, c_out, a_mid, b_mid, c_mid, sem_in, sem_out):
@@ -392,7 +422,6 @@
     n_layers = n_dev // LAYER if fuse_sum else 1
     depth = feat // LAYER + 1
     hbm = pl.BlockSpec(memory_space=pltpu.HBM)
-    vmem = pl.BlockSpec(memory_space=pltpu.VMEM)
     dma = pltpu.SemaphoreType.DMA
     others = max(n_rep - 1, 1)
     act, grad_w, grad_b = pl.pallas_call(
@@ -403,7 +432,7 @@
             jax.ShapeDtypeStruct((1, hidden), jnp.float32),
         ),
         in_specs=[hbm] * 8,
-        out_specs=(vmem, vmem, vmem),
+        out_specs=(hbm, hbm, hbm),
         scratch_shapes=[
             pltpu.VMEM(features.shape, features.dtype),
             pltpu.VMEM((blocks, BLK), degree.dtype),
@@ -413,13 +442,17 @@
             pltpu.VMEM(weight.shape, weight.dtype),
             pltpu.VMEM((1, hidden), bias.dtype),
             pltpu.VMEM(cotangent.shape, cotangent.dtype),
+            pltpu.VMEM((share, hidden), jnp.bfloat16),
+            pltpu.VMEM((1, hidden), jnp.float32),
+            pltpu.VMEM((nodes, feat), jnp.float32),
+            dma((2 + LAYER,)),
             pltpu.VMEM((nodes, feat), jnp.bfloat16),
             pltpu.VMEM((nodes, feat), jnp.float32),
             pltpu.VMEM((steps, nodes, nodes), jnp.bfloat16),
             pltpu.VMEM((steps + 1, nodes, feat), jnp.bfloat16),
             pltpu.VMEM((others, share, feat), jnp.bfloat16),
             pltpu.VMEM((others, share, feat), jnp.bfloat16),
-            pltpu.VMEM((LAYER, depth, hidden), jnp.float32),
+            pltpu.VMEM((LAYER, depth, hidden) if fuse_sum else (1, feat, hidden), jnp.float32),
             pltpu.VMEM((LAYER, depth, hidden), jnp.float32),
             pltpu.VMEM((n_layers, depth, hidden), jnp.float32),
             pltpu.VMEM((LAYER, depth, hidden), jnp.float32),

time: 43.4 us -> 44.4 us (1.023)
  Pallas kernels: 42.6 us -> 43.6 us
    pallas_call x1, Pallas kernels: 41 us -> 41.9 us  [local(): pl.pallas_call(functools.partial(kernel, n_rows, n_rep, fuse_sum), out_sh...]
where the time goes in v6:
time: 44.4 us; the launch traced here: 44.2 us
  Pallas kernels  43.6 us (98%)
  between operations  0.64 us (1%)
    pallas_call x1, Pallas kernels, local(): pl.pallas_call(functools.partial(kernel, n_rows, n_rep, fuse_sum), out_sh...  41.9 us
    pallas_call x1, Pallas kernels, finish(): pl.pallas_call(finish_kernel, out_shape=tuple((jax.ShapeDtypeStruct(r.sha...  1.68 us

profile of v6, /device:TPU:0, one launch (start us, length us, event | category | flops | bytes accessed | tf_op | source)
XLA Modules:
  0.0 44.2 jit_solution(8915545020553488275)
XLA Ops:
  0.6 41.9 %shard_map.103 = (bf16[256,256]{1,0:T(8,128)(2,1)}, f32[128,256]{1,0:T(8,128)}, f32[1,256]{1,0:T(1,128)}) custom-call(bf16[512,128]{1,0:T(8,128)(2,1)} %feat_hbm.1, s32[4,128]{1,0:T(4,128)} %bitcast.3, s32[4,8,8]{2,1,0:T(8,128)} %tb_hbm.1, s32[4,8,8]{2,1,0:T(8,128)} %cnt_hbm.1, s32[4,8,8,128]{3,2,1,0:T(8,128)} %code_hbm.1, bf16[128,256]{1,0:T(8,128)(2,1)} %w_hbm.1, ...), custom_call_target="tpu_custom_call" | custom-call | tf_op jit(solution)/shard_map/pallas_call | solution.py:427
  42.6 1.7 %shard_map.104 = (bf16[256,256]{1,0:T(8,128)(2,1)}, f32[128,256]{1,0:T(8,128)}, f32[1,256]{1,0:T(1,128)}) custom-call(bf16[256,256]{1,0:T(8,128)(2,1)} %get-tuple-element.9.a_ref, f32[128,256]{1,0:T(8,128)} %get-tuple-element.10.b_ref, f32[1,256]{1,0:T(1,128)} %get-tuple-element.11.c_ref), custom_call_target="tpu_custom_call" | custom-call | tf_op jit(solution)/shard_map/pallas_call | solution.py:402

commit v7 on v5

--- a/solution.py
+++ b/solution.py
@@ -210,11 +210,12 @@
         adj[o, pl.ds(pl.multiple_of(i * BLK, BLK), BLK), :] = tile.astype(jnp.bfloat16)
 
     total_steps = blocks * steps
-    cuts = (0, total_steps * 3 // 8, total_steps * 11 // 16, total_steps)
+    cuts = (0, total_steps // 8 * 3, total_steps // 16 * 11, total_steps)
     for part_index, ready in enumerate(((1,), (0, 2), ())):
-        @pl.loop(cuts[part_index], cuts[part_index + 1])
+        @pl.loop(cuts[part_index] // 2, cuts[part_index + 1] // 2)
         def _(t):
-            build(t)
+            build(2 * t)
+            build(2 * t + 1)
 
         for t in ready:
             land(t)

time: 43.4 us -> 43 us (level)
    pallas_call x1, Pallas kernels: 41 us -> 40.5 us  [local(): pl.pallas_call(functools.partial(kernel, n_rows, n_rep, fuse_sum), out_sh...]
where the time goes in v7:
time: 43 us; the launch traced here: 42.8 us
  Pallas kernels  42.2 us (98%)
  between operations  0.64 us (1%)
    pallas_call x1, Pallas kernels, local(): pl.pallas_call(functools.partial(kernel, n_rows, n_rep, fuse_sum), out_sh...  40.5 us
    pallas_call x1, Pallas kernels, finish(): pl.pallas_call(finish_kernel, out_shape=tuple((jax.ShapeDtypeStruct(r.sha...  1.68 us

profile of v7, /device:TPU:0, one launch (start us, length us, event | category | flops | bytes accessed | tf_op | source)
XLA Modules:
  0.0 42.8 jit_solution(13330862969349432678)
XLA Ops:
  0.6 40.5 %shard_map.103 = (bf16[256,256]{1,0:T(8,128)(2,1)}, f32[128,256]{1,0:T(8,128)}, f32[1,256]{1,0:T(1,128)}) custom-call(bf16[512,128]{1,0:T(8,128)(2,1)} %feat_hbm.1, s32[4,128]{1,0:T(4,128)} %bitcast.3, s32[4,8,8]{2,1,0:T(8,128)} %tb_hbm.1, s32[4,8,8]{2,1,0:T(8,128)} %cnt_hbm.1, s32[4,8,8,128]{3,2,1,0:T(8,128)} %code_hbm.1, bf16[128,256]{1,0:T(8,128)(2,1)} %w_hbm.1, ...), custom_call_target="tpu_custom_call" | custom-call | tf_op jit(solution)/shard_map/pallas_call | solution.py:399
  41.1 1.7 %shard_map.104 = (bf16[256,256]{1,0:T(8,128)(2,1)}, f32[128,256]{1,0:T(8,128)}, f32[1,256]{1,0:T(1,128)}) custom-call(bf16[256,256]{1,0:T(8,128)(2,1)} %get-tuple-element.9.a_ref, f32[128,256]{1,0:T(8,128)} %get-tuple-element.10.b_ref, f32[1,256]{1,0:T(1,128)} %get-tuple-element.11.c_ref), custom_call_target="tpu_custom_call" | custom-call | tf_op jit(solution)/shard_map/pallas_call | solution.py:373

commit v8 on v7

--- a/solution.py
+++ b/solution.py
@@ -20,8 +20,9 @@
     feat_hbm, deg_hbm, tb_hbm, cnt_hbm, code_hbm, w_hbm, b_hbm, cot_hbm,
     act_ref, gw_ref, gb_ref,
     feat_ref, deg_ref, tb_ref, cnt_ref, code_ref, w_ref, b_ref, cot_ref,
-    own, invb, adj, gathered, part, precv, gwp, grecv, zrecv, gfin,
+    own, invb, adj, gathered, part, precv, gwp, grecv, zrecv, gfin, bl, bz,
     in_sem, d_send, f_send, s_recv, p_send, p_recv, g_send, g_recv, z_send, z_recv, o_send, o_recv,
+    bl_send, bl_recv, bz_send, bz_recv,
 ):
     blocks, steps, slots, ecap = code_ref.shape
     nodes = blocks * BLK
@@ -289,8 +290,28 @@
 
     depth = weight_sum.shape[0] // LAYER
     for p in range(LAYER):
-        gwp[p, 0:depth, :] = weight_sum[p * depth : (p + 1) * depth, :]
-        gwp[p, depth : depth + 1, :] = bias_sum
+        gwp[p] = weight_sum[p * depth : (p + 1) * depth, :].astype(jnp.bfloat16)
+    bl[place] = bias_sum
+
+    def tell(d):
+        return pltpu.make_async_remote_copy(
+            src_ref=bl.at[place],
+            dst_ref=bl.at[place],
+            send_sem=bl_send.at[d - 1],
+            recv_sem=bl_recv.at[d - 1],
+            device_id=layer_peer(d)[1],
+            device_id_type=MESH,
+        )
+
+    def tell_layers(d):
+        return pltpu.make_async_remote_copy(
+            src_ref=bz.at[layer],
+            dst_ref=bz.at[layer],
+            send_sem=bz_send.at[d - 1],
+            recv_sem=bz_recv.at[d - 1],
+            device_id=layer_at(d)[1],
+            device_id_type=MESH,
+        )
 
     def scatter(d):
         at, device = layer_peer(d)
@@ -325,32 +346,49 @@
 
     for d in range(1, LAYER):
         scatter(d).start()
+    for d in range(1, LAYER):
+        tell(d).start()
     grecv[place] = gwp[place]
     for d in range(1, LAYER):
         scatter(d).wait_recv()
-    total = grecv[0]
+    total = grecv[0].astype(jnp.float32)
     for s in range(1, LAYER):
-        total = total + grecv[s]
-    zrecv[layer] = total
+        total = total + grecv[s].astype(jnp.float32)
+    zrecv[layer] = total.astype(jnp.bfloat16)
     for d in range(1, n_layers):
         swap(d).start()
+    for d in range(1, LAYER):
+        tell(d).wait_recv()
+    bias_total = bl[0]
+    for s in range(1, LAYER):
+        bias_total = bias_total + bl[s]
+    bz[layer] = bias_total
+    for d in range(1, n_layers):
+        tell_layers(d).start()
     for d in range(1, n_layers):
         swap(d).wait_recv()
-    total = zrecv[0]
+    total = zrecv[0].astype(jnp.float32)
     for s in range(1, n_layers):
-        total = total + zrecv[s]
+        total = total + zrecv[s].astype(jnp.float32)
     gfin[place] = total
     for d in range(1, LAYER):
         spread(d).start()
-    gb_ref[...] = total[depth : depth + 1, :]
+    for d in range(1, n_layers):
+        tell_layers(d).wait_recv()
+    bias_total = bz[0]
+    for s in range(1, n_layers):
+        bias_total = bias_total + bz[s]
+    gb_ref[...] = bias_total
     for d in range(1, LAYER):
         scatter(d).wait_send()
+        tell(d).wait_send()
     for d in range(1, n_layers):
         swap(d).wait_send()
+        tell_layers(d).wait_send()
     for d in range(1, LAYER):
         spread(d).wait_recv()
     for p in range(LAYER):
-        gw_ref[p * depth : (p + 1) * depth, :] = gfin[p, 0:depth, :]
+        gw_ref[p * depth : (p + 1) * depth, :] = gfin[p]
     for d in range(1, LAYER):
         spread(d).wait_send()
 
@@ -391,7 +429,7 @@
     share = nodes // n_rep
     fuse_sum = n_dev % LAYER == 0 and n_dev <= 8 * LAYER and LAYER % n_rep == 0 and feat % (8 * LAYER) == 0
     n_layers = n_dev // LAYER if fuse_sum else 1
-    depth = feat // LAYER + 1
+    depth = feat // LAYER
     hbm = pl.BlockSpec(memory_space=pltpu.HBM)
     vmem = pl.BlockSpec(memory_space=pltpu.VMEM)
     dma = pltpu.SemaphoreType.DMA
@@ -420,10 +458,12 @@
             pltpu.VMEM((steps + 1, nodes, feat), jnp.bfloat16),
             pltpu.VMEM((others, share, feat), jnp.bfloat16),
             pltpu.VMEM((others, share, feat), jnp.bfloat16),
+            pltpu.VMEM((LAYER, depth, hidden), jnp.bfloat16),
+            pltpu.VMEM((LAYER, depth, hidden), jnp.bfloat16),
+            pltpu.VMEM((n_layers, depth, hidden), jnp.bfloat16),
             pltpu.VMEM((LAYER, depth, hidden), jnp.float32),
-            pltpu.VMEM((LAYER, depth, hidden), jnp.float32),
-            pltpu.VMEM((n_layers, depth, hidden), jnp.float32),
-            pltpu.VMEM((LAYER, depth, hidden), jnp.float32),
+            pltpu.VMEM((LAYER, 1, hidden), jnp.float32),
+            pltpu.VMEM((n_layers, 1, hidden), jnp.float32),
             dma((8,)),
             dma((3,)),
             dma((3 * SEATS,)),
@@ -436,6 +476,10 @@
             dma((max(n_layers - 1, 1),)),
             dma((LAYER - 1,)),
             dma((LAYER - 1,)),
+            dma((LAYER - 1,)),
+            dma((LAYER - 1,)),
+            dma((max(n_layers - 1, 1),)),
+            dma((max(n_layers - 1, 1),)),
         ],
         compiler_params=pltpu.CompilerParams(
             collective_id=0, has_side_effects=True, vmem_limit_bytes=65000 * 1024

time: 43 us -> 40.6 us (0.944)
  Pallas kernels: 42.2 us -> 39.8 us
    pallas_call x1, Pallas kernels: 40.5 us -> 38.1 us  [local(): pl.pallas_call(functools.partial(kernel, n_rows, n_rep, fuse_sum), out_sh...]
where the time goes in v8:
time: 40.6 us; the launch traced here: 40.4 us
  Pallas kernels  39.8 us (98%)
  between operations  0.64 us (2%)
    pallas_call x1, Pallas kernels, local(): pl.pallas_call(functools.partial(kernel, n_rows, n_rep, fuse_sum), out_sh...  38.1 us
    pallas_call x1, Pallas kernels, finish(): pl.pallas_call(finish_kernel, out_shape=tuple((jax.ShapeDtypeStruct(r.sha...  1.68 us

profile of v8, /device:TPU:0, one launch (start us, length us, event | category | flops | bytes accessed | tf_op | source)
XLA Modules:
  0.0 40.4 jit_solution(13976421155364785215)
XLA Ops:
  0.6 38.1 %shard_map.103 = (bf16[256,256]{1,0:T(8,128)(2,1)}, f32[128,256]{1,0:T(8,128)}, f32[1,256]{1,0:T(1,128)}) custom-call(bf16[512,128]{1,0:T(8,128)(2,1)} %feat_hbm.1, s32[4,128]{1,0:T(4,128)} %bitcast.3, s32[4,8,8]{2,1,0:T(8,128)} %tb_hbm.1, s32[4,8,8]{2,1,0:T(8,128)} %cnt_hbm.1, s32[4,8,8,128]{3,2,1,0:T(8,128)} %code_hbm.1, bf16[128,256]{1,0:T(8,128)(2,1)} %w_hbm.1, ...), custom_call_target="tpu_custom_call" | custom-call | tf_op jit(solution)/shard_map/pallas_call | solution.py:437
  38.7 1.7 %shard_map.104 = (bf16[256,256]{1,0:T(8,128)(2,1)}, f32[128,256]{1,0:T(8,128)}, f32[1,256]{1,0:T(1,128)}) custom-call(bf16[256,256]{1,0:T(8,128)(2,1)} %get-tuple-element.9.a_ref, f32[128,256]{1,0:T(8,128)} %get-tuple-element.10.b_ref, f32[1,256]{1,0:T(1,128)} %get-tuple-element.11.c_ref), custom_call_target="tpu_custom_call" | custom-call | tf_op jit(solution)/shard_map/pallas_call | solution.py:411
